TPU v7x, 32 devices: a whole 2x2x4 slice. The times are simulated.
32 devices in a mesh: tp: 4 (over x, core), ad: 8 (over z, y).
Axes of the slice: x: 2, y: 2, z: 4, core: 2. Of those that a mesh axis runs over, the one named last changes fastest.
Arguments:
- hidden: bfloat16 [3584, 8192], P('ad'), may hold values from -6 to 6
- gain: bfloat16 [8192], replicated, may hold values from 0.25 to 1.75
- key_value_weight: bfloat16 [8192, 2, 1024], P(None, None, 'tp'), may hold values from -0.0625 to 0.0625
- adapter_down_weight: bfloat16 [16, 8192, 128], P('ad', 'tp'), may hold values from -0.0625 to 0.0625
- adapter_up_weight: bfloat16 [16, 2, 64, 1024], P('ad', None, None, 'tp'), may hold values from -0.75 to 0.75
- language_pair_index: int32 [3584], P('ad'), may hold values from 0 to 15, as said below
- adapter_row_index: int32 [16], replicated, may hold values from 0 to 15, as said below
Outputs:
- kv_out: bfloat16 [3584, 2, 1024], P('ad', None, 'tp')
Inputs may be any that keep to these rules, and one draw needn't show every extreme that they name: A row's owner is adapter_row_index[language_pair_index] // 2. Among the rows of one device, one owner, the same for every device, has exactly 224 rows; every other owner has at most 112, and one other owner, the same for every device, exactly 112. `adapter_row_index`: each adapter's row in adapter_down_weight and adapter_up_weight; every row appears once.
All inputs are finite; a program needn't handle non-finite values.
Results may differ from a plain program's by a relative error of at most 0.0053.
Values may be sent and summed in bfloat16 or wider, within the bound.
A program may use at most 128 MiB of HBM per device.

v0:
```python
import jax
import jax.numpy as jnp
from jax import lax
from jax.sharding import PartitionSpec as P

epsilon = 1e-05
adapter_scale = 0.5


def down_local(rows_in, row_ids, down_table):
    adapter_total = down_table.shape[0]
    labels = jnp.arange(adapter_total, dtype=jnp.int32)
    row_mask = row_ids[:, None] == labels[None, :]
    every_low = jnp.einsum("rc,acm->ram", rows_in, down_table, preferred_element_type=jnp.float32)
    partial_low = jnp.sum(jnp.where(row_mask[:, :, None], every_low, jnp.float32(0.0)), axis=1)
    return (partial_low, row_mask)


def upward_delta(summed_low, row_mask, up_table):
    narrow = summed_low.astype(jnp.bfloat16)
    row_total = narrow.shape[0]
    adapter_total = up_table.shape[0]
    rank_width = up_table.shape[2]
    widened = jnp.where(row_mask[:, :, None], narrow[:, None, :], jnp.zeros((), jnp.bfloat16))
    widened = widened.reshape(row_total, adapter_total, 2, rank_width)
    values = jnp.einsum("racq,acqh->rch", widened, up_table, preferred_element_type=jnp.float32)
    return values.astype(jnp.bfloat16)


def on_device(
    hidden,
    gain,
    key_value_weight,
    adapter_down_weight,
    adapter_up_weight,
    language_pair_index,
    adapter_row_index,
):
    tok_count = hidden.shape[0]
    model_width = hidden.shape[1]
    owner_count = lax.axis_size("ad")
    by_holder = adapter_down_weight.shape[0]
    column_portion = adapter_down_weight.shape[1]
    head_cols = key_value_weight.shape[2]
    row_quota = tok_count // owner_count
    wide_hidden = hidden.astype(jnp.float32)
    inv_rms = lax.rsqrt(jnp.mean(wide_hidden * wide_hidden, axis=-1, keepdims=True) + epsilon)
    normed = (wide_hidden * inv_rms * gain.astype(jnp.float32)).astype(jnp.bfloat16)
    base_projection = jnp.dot(
        normed,
        key_value_weight.reshape(model_width, 2 * head_cols),
        preferred_element_type=jnp.float32,
    ).reshape(tok_count, 2, head_cols)
    own_cols = lax.dynamic_slice_in_dim(
        normed, lax.axis_index("tp") * column_portion, column_portion, 1
    )
    slot_ids = adapter_row_index[language_pair_index]
    owner_ids = slot_ids // by_holder
    local_ids = slot_ids % by_holder
    owner_labels = jnp.arange(owner_count, dtype=jnp.int32)
    capacity = 4 * row_quota
    onehot = (owner_ids[:, None] == owner_labels[None, :]).astype(jnp.int32)
    before = jnp.cumsum(onehot, axis=0) - onehot
    bucket_pos = jnp.sum(before * onehot, axis=1)
    total_slots = owner_count * capacity
    dest_slot = jnp.where(owner_ids < owner_count, owner_ids * capacity + bucket_pos, total_slots)
    slot_labels = jnp.arange(total_slots, dtype=jnp.int32)
    selector = slot_labels[:, None] == dest_slot[None, :]
    selector_bf = selector.astype(jnp.bfloat16)
    send_rows = jnp.dot(selector_bf, own_cols, preferred_element_type=jnp.float32).astype(
        jnp.bfloat16
    )
    send_rows = send_rows.reshape(owner_count, capacity, column_portion)
    filled = jnp.any(selector, axis=1)
    picked_ids = jnp.sum(jnp.where(selector, local_ids[None, :], 0), axis=1)
    send_ids = jnp.where(filled, picked_ids, by_holder).reshape(owner_count, capacity)
    received_rows = lax.all_to_all(send_rows, "ad", split_axis=0, concat_axis=0, tiled=True)
    got_ids = lax.all_to_all(send_ids, "ad", split_axis=0, concat_axis=0, tiled=True)
    source_count = got_ids.shape[0]
    element_count = got_ids.shape[1]
    flat_ids = got_ids.reshape(source_count * element_count)
    partial_low, row_mask = down_local(
        received_rows.reshape(source_count * element_count, column_portion),
        flat_ids,
        adapter_down_weight,
    )
    summed_output = lax.psum(partial_low, "tp")
    delta_rows = upward_delta(summed_output, row_mask, adapter_up_weight).reshape(
        source_count, element_count, 2, head_cols
    )
    returned = lax.all_to_all(delta_rows, "ad", split_axis=0, concat_axis=0, tiled=True)
    flat_back = returned.reshape(total_slots, 2 * head_cols)
    back_rows = jnp.einsum("st,sc->tc", selector_bf, flat_back, preferred_element_type=jnp.float32)
    delta_by_row = back_rows.astype(jnp.bfloat16).reshape(tok_count, 2, head_cols)
    return (base_projection + adapter_scale * delta_by_row.astype(jnp.float32)).astype(jnp.bfloat16)


def solution(mesh):
    return jax.shard_map(
        on_device,
        mesh=mesh,
        in_specs=(
            P("ad", None),
            P(),
            P(None, None, "tp"),
            P("ad", "tp", None),
            P("ad", None, None, "tp"),
            P("ad"),
            P(),
        ),
        out_specs=P("ad", None, "tp"),
        check_vma=False,
    )
```

profile of v0, /device:TPU:0, one launch (start us, length us, event | category | flops | bytes accessed | tf_op | source)
XLA Modules:
  0.0 297.3 jit_solution(16910015421758755141)
XLA Ops:
  0.0 0.0 copy-start
  0.0 0.0 copy-start.3
  0.0 2.0 fusion.30
  2.0 10.6 %add_select_fusion = (s32[448]{0:T(512)S(1)}, s32[448]{0:T(512)S(1)}) fusion(s32[]{:T(128)} %bitcast.18, s32[]{:T(128)} %bitcast.17, s32[]{:T(128)} %bitcast.16, s32[]{:T(128)} %bitcast.15, s32[]{:T(128)} %bitcast.14, s32[]{:T(128)} %bitcast.13, s32[]{:T(128)} %bitcast.12, s32[]{:T(128)} %bitcast.11, s32[]{:T(128)} %bitcast.10, s32[]{:T(128)} %bitcast.9, ...), kind=kLoop, calls=%fused_computation.39 | loop fusion | flops 19712 | bytes 5440 | tf_op jit(solution)/shard_map/jit(remainder)/select_n | solution.py:59
  12.6 1.1 reduce-window.6
  13.8 0.2 slice_reduce_fusion
  14.0 0.1 add_bitcast_fusion
  14.2 0.6 fusion.6
  14.7 0.4 select_reduce_fusion
  15.2 0.7 select_n.72
  15.9 7.3 %all-to-all-start = ((s32[8,1,224]{2,1,0:T(1,128)}), s32[8,1,224]{2,1,0:T(1,128)S(1)}, u32[]{:S(2)}, u32[]{:S(2)}) async-start(s32[8,1,224]{2,1,0:T(1,128)} %select_n.72), calls=%async_computation | async-start | bytes 16384 | tf_op jit(solution)/shard_map/all_to_all | solution.py:78
  23.1 4.6 %fusion = f32[448]{0:T(512)S(1)} fusion(bf16[448,8192]{1,0:T(8,128)(2,1)} %param.7), kind=kLoop, calls=%fused_computation.2 | loop fusion | flops 11009600 | bytes 7341824 | tf_op jit(solution)/shard_map/reduce_sum | solution.py:47
  27.8 0.0 copy-done.3
  27.8 5.5 %fusion.2 = bf16[448,8192]{1,0:T(8,128)(2,1)S(1)} fusion(bf16[448,8192]{1,0:T(8,128)(2,1)} %param.7, f32[8192]{0:T(1024)S(1)} %convert_element_type.37, f32[448]{0:T(512)S(1)} %add_rsqrt_fusion), kind=kLoop, calls=%fused_computation.4 | loop fusion | flops 14680064 | bytes 14714624 | tf_op jit(solution)/shard_map/convert_element_type | solution.py:48
  33.3 0.0 copy-start.2
  33.3 3.0 copy-done.2
  36.3 6.4 %convolution_convert_fusion = bf16[1792,2048]{1,0:T(8,128)(2,1)} fusion(bf16[448,8192]{1,0:T(8,128)(2,1)S(1)} %fusion.2, s32[]{:T(128)S(6)} %select_n.73, s32[448]{0:T(512)S(1)} %add_select_fusion.2), kind=kOutput, calls=%fused_computation.5 | convolution fusion | flops 3292807168 | bytes 9177092 | tf_op jit(solution)/shard_map/dot_general | solution.py:70
  42.6 0.0 all-to-all-done
  42.6 6.0 %all-to-all-start.1 = ((bf16[8,224,2048]{2,1,0:T(8,128)(2,1)}), bf16[8,224,2048]{2,1,0:T(8,128)(2,1)}, u32[]{:S(2)}, u32[]{:S(2)}) async-start(bf16[8,224,2048]{2,1,0:T(8,128)(2,1)} %bitcast.58), calls=%async_computation.1 | async-start | bytes 14680064 | tf_op jit(solution)/shard_map/all_to_all | solution.py:77
  48.6 0.1 eq.63
  48.7 160.0 %all-to-all-done.1 = bf16[8,224,2048]{2,1,0:T(8,128)(2,1)} async-done(((bf16[8,224,2048]{2,1,0:T(8,128)(2,1)}), bf16[8,224,2048]{2,1,0:T(8,128)(2,1)}, u32[]{:S(2)}, u32[]{:S(2)}) %all-to-all-start.1) | async-done | bytes 7340064 | tf_op jit(solution)/shard_map/all_to_all | solution.py:77
  208.7 0.0 copy-done
  208.8 0.0 copy-start.4
  208.8 5.3 %fusion.10 = f32[1792,128]{1,0:T(8,128)S(1)} fusion(bf16[1792,2048,1]{1,0,2:T(8,128)(2,1)} %bitcast.24, bf16[2,2048,128]{2,1,0:T(8,128)(2,1)S(1)} %copy-done, pred[1792,2]{0,1:T(4,128)(4,1)S(1)} %iota_compare_fusion.11), kind=kOutput, calls=%fused_computation.17 | convolution fusion | flops 1879736320 | bytes 9309696 | tf_op jit(solution)/shard_map/rc,acm->ram/dot_general | solution.py:14
  214.1 20.9 %all-reduce.2 = bf16[1792,128]{1,0:T(8,128)(2,1)S(1)} all-reduce(f32[1792,128]{1,0:T(8,128)S(1)} %fusion.10), channel_id=1, replica_groups=mesh['tp'=4,'ad'=8] {'tp'}, use_global_device_ids=true, to_apply=%region_7.8 | all-reduce | flops 229376 | bytes 1376256 | tf_op jit(solution)/shard_map/psum | solution.py:87
  235.0 0.2 copy.29
  235.2 0.0 copy-done.4
  235.2 0.7 bitcast_convert_fusion
  235.9 3.2 %copy.31 = bf16[8,224,2,256]{3,2,1,0:T(2,128)(2,1)} copy(bf16[8,224,2,256]{3,1,0,2:T(8,128)(2,1)S(1)} %bitcast.60) | data formatting | bytes 3670016 | tf_op jit(solution)/shard_map/reshape | solution.py:88
  239.1 4.1 %all-to-all-start.2 = ((bf16[8,224,2,256]{3,2,1,0:T(2,128)(2,1)}), bf16[8,224,2,256]{3,2,1,0:T(2,128)(2,1)S(1)}, u32[]{:S(2)}, u32[]{:S(2)}) async-start(bf16[8,224,2,256]{3,2,1,0:T(2,128)(2,1)} %copy.31), calls=%async_computation.2 | async-start | bytes 3670016 | tf_op jit(solution)/shard_map/all_to_all | solution.py:91
  243.2 8.0 %copy.36 = bf16[1024,8,2,256]{3,1,2,0:T(8,128)(2,1)} copy(bf16[1024,8,2,256]{3,2,1,0:T(2,128)(2,1)} %bitcast.56) | data formatting | bytes 16777216
  251.2 11.4 %copy.28 = bf16[512,8192]{1,0:T(8,128)(2,1)} copy(bf16[512,8192]{0,1:T(8,128)(2,1)} %bitcast.55) | data formatting | bytes 16777216 | tf_op jit(solution)/shard_map/dot_general | solution.py:49
  262.6 23.5 %all-to-all-done.2 = bf16[8,224,2,256]{3,2,1,0:T(2,128)(2,1)S(1)} async-done(((bf16[8,224,2,256]{3,2,1,0:T(2,128)(2,1)}), bf16[8,224,2,256]{3,2,1,0:T(2,128)(2,1)S(1)}, u32[]{:S(2)}, u32[]{:S(2)}) %all-to-all-start.2) | async-done | bytes 1835040 | tf_op jit(solution)/shard_map/all_to_all | solution.py:91
  286.1 0.0 copy-start.1
  286.1 0.4 copy.37
  286.5 1.0 fusion.13
  287.5 1.9 copy-done.1
  289.5 6.5 %fusion.17 = bf16[448,2,256]{2,0,1:T(8,128)(2,1)S(1)} fusion(bf16[2,256,8192]{2,1,0:T(8,128)(2,1)S(1)} %bitcast.57, bf16[448,8192]{1,0:T(8,128)(2,1)} %copy-done.2, f32[56,2,8,256]{3,2,1,0:T(8,128)S(1)} %bitcast.63), kind=kOutput, calls=%fused_computation.22 | convolution fusion | flops 3758555136 | bytes 17104896 | tf_op jit(solution)/shard_map/dot_general | solution.py:49
  296.0 1.2 copy.33
  (12 shorter events, 0.2 us)
Async XLA Ops:
  0.0 208.7 %copy-start = (bf16[2,2048,128]{2,1,0:T(8,128)(2,1)S(1)}, bf16[2,2048,128]{2,1,0:T(8,128)(2,1)}, u32[]{:S(2)}) copy-start(bf16[2,2048,128]{2,1,0:T(8,128)(2,1)} %param.10) | copy-start | bytes 3145732
  0.0 27.8 %copy-start.3 = (bf16[8192]{0:T(1024)(128)(2,1)S(1)}, bf16[8192]{0:T(1024)(128)(2,1)}, u32[]{:S(2)}) copy-start(bf16[8192]{0:T(1024)(128)(2,1)} %param.8) | copy-start | bytes 49156
  15.9 26.7 %all-to-all-start = ((s32[8,1,224]{2,1,0:T(1,128)}), s32[8,1,224]{2,1,0:T(1,128)S(1)}, u32[]{:S(2)}, u32[]{:S(2)}) async-start(s32[8,1,224]{2,1,0:T(1,128)} %select_n.72), calls=%async_computation | async-start | bytes 16384 | tf_op jit(solution)/shard_map/all_to_all | solution.py:78
  33.3 3.0 copy-start.2
  42.6 166.1 %all-to-all-start.1 = ((bf16[8,224,2048]{2,1,0:T(8,128)(2,1)}), bf16[8,224,2048]{2,1,0:T(8,128)(2,1)}, u32[]{:S(2)}, u32[]{:S(2)}) async-start(bf16[8,224,2048]{2,1,0:T(8,128)(2,1)} %bitcast.58), calls=%async_computation.1 | async-start | bytes 14680064 | tf_op jit(solution)/shard_map/all_to_all | solution.py:77
  208.8 26.4 %copy-start.4 = (bf16[2,2,64,256]{3,2,1,0:T(8,128)(2,1)S(1)}, bf16[2,2,64,256]{3,2,1,0:T(8,128)(2,1)}, u32[]{:S(2)}) copy-start(bf16[2,2,64,256]{3,2,1,0:T(8,128)(2,1)} %param.11) | copy-start | bytes 393220
  239.1 47.0 %all-to-all-start.2 = ((bf16[8,224,2,256]{3,2,1,0:T(2,128)(2,1)}), bf16[8,224,2,256]{3,2,1,0:T(2,128)(2,1)S(1)}, u32[]{:S(2)}, u32[]{:S(2)}) async-start(bf16[8,224,2,256]{3,2,1,0:T(2,128)(2,1)} %copy.31), calls=%async_computation.2 | async-start | bytes 3670016 | tf_op jit(solution)/shard_map/all_to_all | solution.py:91
  286.1 3.4 %copy-start.1 = (bf16[512,8192]{1,0:T(8,128)(2,1)S(1)}, bf16[512,8192]{1,0:T(8,128)(2,1)}, u32[]{:S(2)}) copy-start(bf16[512,8192]{1,0:T(8,128)(2,1)} %copy.28) | copy-start | bytes 25165828
where the time goes:
time: 298 us; the launch traced here: 297 us
  waiting for transfers between devices  184 us (62%)
  local copies, waits for them, and re-layouts  32.3 us (11%)
  other arithmetic  23.1 us (8%)
  blocking collectives  20.9 us (7%)
  matrix products  19.9 us (7%)
  starting transfers between devices  17.4 us (6%)
    all_to_all x1, waiting for transfers between devices, on_device(): lax.all_to_all(send_rows, 'ad', split_axis=0, concat_axis=0, tiled=True)  160 us
    all_to_all x1, waiting for transfers between devices, on_device(): lax.all_to_all(delta_rows, 'ad', split_axis=0, concat_axis=0, tiled=True)  23.5 us
    psum x1, blocking collectives, on_device(): summed_output = lax.psum(partial_low, 'tp')  20.9 us
    unnamed x12, local copies, waits for them, and re-layouts  13.3 us
    dot_general x1, local copies, waits for them, and re-layouts, on_device(): jnp.dot(normed, key_value_weight.reshape(model_width, 2 * head_cols), pre...  11.4 us
    select_n x1, other arithmetic, on_device(): local_ids = slot_ids % by_holder  10.6 us
    all_to_all x1, starting transfers between devices, on_device(): lax.all_to_all(send_ids, 'ad', split_axis=0, concat_axis=0, tiled=True)  7.28 us
    dot_general x1, matrix products, on_device(): jnp.dot(normed, key_value_weight.reshape(model_width, 2 * head_cols), pre...  6.54 us
  transfers between devices with their start and end apart: 3, of which 2 were waited for; matrix products, arithmetic and copies ran while one was open for 12% of the time, Pallas kernels for 0%

commit v1 on v0

v1 whole, which is shorter than its diff:
```python
import jax
import jax.numpy as jnp
from jax import lax
from jax.sharding import PartitionSpec as P

epsilon = 1e-05
adapter_scale = 0.5


def ring_order(count):
    return list(range(0, count, 2)) + list(reversed(range(1, count, 2)))


def on_device(
    hidden,
    gain,
    key_value_weight,
    adapter_down_weight,
    adapter_up_weight,
    language_pair_index,
    adapter_row_index,
):
    tok_count, model_width = hidden.shape
    owners = lax.axis_size("ad")
    held, column_portion, low_width = adapter_down_weight.shape
    head_cols = key_value_weight.shape[2]
    rank = adapter_up_weight.shape[2]
    me = lax.axis_index("ad")

    order = ring_order(owners)
    forward = [(order[i], order[(i + 1) % owners]) for i in range(owners)]
    backward = [(b, a) for a, b in forward]
    place = [order.index(i) for i in range(owners)]
    my_place = jnp.asarray(place, jnp.int32)[me]
    order_table = jnp.asarray(order, jnp.int32)

    up_all = lax.all_gather(adapter_up_weight, "ad", axis=0, tiled=True)

    wide_hidden = hidden.astype(jnp.float32)
    inv_rms = lax.rsqrt(jnp.mean(wide_hidden * wide_hidden, axis=-1, keepdims=True) + epsilon)
    normed = (wide_hidden * inv_rms * gain.astype(jnp.float32)).astype(jnp.bfloat16)
    own_cols = lax.dynamic_slice_in_dim(
        normed, lax.axis_index("tp") * column_portion, column_portion, 1
    )
    slot_ids = adapter_row_index[language_pair_index]

    def term(block, first_id):
        total = jnp.zeros((tok_count, low_width), jnp.float32)
        for j in range(block.shape[0]):
            low = jnp.dot(own_cols, block[j], preferred_element_type=jnp.float32)
            total = total + jnp.where((slot_ids == first_id + j)[:, None], low, jnp.float32(0.0))
        return total

    low = term(adapter_down_weight, me * held)
    up_block = down_block = adapter_down_weight
    half = held // 2
    for step in range(1, owners // 2 + 1):
        from_behind = order_table[lax.rem(my_place + owners - step, owners)]
        from_ahead = order_table[lax.rem(my_place + step, owners)]
        if step < owners // 2:
            up_block = lax.ppermute(up_block, "ad", forward)
            down_block = lax.ppermute(down_block, "ad", backward)
            low = low + term(up_block, from_behind * held) + term(down_block, from_ahead * held)
        else:
            first = lax.ppermute(up_block[:half], "ad", forward)
            rest = lax.ppermute(down_block[half:], "ad", backward)
            low = low + term(first, from_behind * held) + term(rest, from_ahead * held + half)

    low_rank = lax.psum(low, "tp").astype(jnp.bfloat16)
    base = jnp.dot(
        normed,
        key_value_weight.reshape(model_width, 2 * head_cols),
        preferred_element_type=jnp.float32,
    ).reshape(tok_count, 2, head_cols)

    adapters = up_all.shape[0]
    mask = slot_ids[:, None] == jnp.arange(adapters, dtype=jnp.int32)[None, :]
    halves = []
    for c in range(2):
        part = low_rank[:, c * rank : (c + 1) * rank]
        wide = jnp.where(mask[:, :, None], part[:, None, :], jnp.zeros((), jnp.bfloat16))
        halves.append(
            jnp.dot(
                wide.reshape(tok_count, adapters * rank),
                up_all[:, c].reshape(adapters * rank, head_cols),
                preferred_element_type=jnp.float32,
            )
        )
    delta = jnp.stack(halves, axis=1).astype(jnp.bfloat16)
    return (base + adapter_scale * delta.astype(jnp.float32)).astype(jnp.bfloat16)


def solution(mesh):
    return jax.shard_map(
        on_device,
        mesh=mesh,
        in_specs=(
            P("ad", None),
            P(),
            P(None, None, "tp"),
            P("ad", "tp", None),
            P("ad", None, None, "tp"),
            P("ad"),
            P(),
        ),
        out_specs=P("ad", None, "tp"),
        check_vma=False,
    )
```

time: 298 us -> 157 us (0.53)
  waiting for transfers between devices: 184 us -> 14.7 us
  between operations: 0.16 us -> 22.8 us
  matrix products: 19.9 us -> 42.5 us
  blocking collectives: 20.9 us -> 12.5 us
  starting transfers between devices: 17.4 us -> 9.58 us
  local copies, waits for them, and re-layouts: 32.3 us -> 28.6 us
    all_to_all x3 -> x0, waiting for transfers between devices: 184 us -> none  [the longest x1 160 us: on_device(): lax.all_to_all(send_rows, 'ad', split_axis=0, concat_axis=0, tiled=True)]
    dot_general x4 -> x18, matrix products: 13.4 us -> 33.1 us  [the longest x16 30 us: term(): low = jnp.dot(own_cols, block[j], preferred_element_type=jnp.float32)]
    all_to_all x3 -> x0, starting transfers between devices: 17.4 us -> none  [the longest x1 7.28 us: on_device(): lax.all_to_all(send_ids, 'ad', split_axis=0, concat_axis=0, tiled=True)]
    ppermute x0 -> x8, waiting for transfers between devices: none -> 14.7 us  [the longest x3 11.2 us: on_device(): down_block = lax.ppermute(down_block, 'ad', backward)]
    select_n x4 -> x1, other arithmetic: 10.7 us -> 0.14 us  [on_device(): jnp.where(mask[:, :, None], part[:, None, :], jnp.zeros((), jnp.bfloat16))]
    eq x2 -> x3, other arithmetic: 0.02 us -> 10.1 us  [the longest x2 10.1 us: term(): slot_ids == first_id + j]
    ppermute x0 -> x8, starting transfers between devices: none -> 9.58 us  [the longest x3 6.95 us: on_device(): down_block = lax.ppermute(down_block, 'ad', backward)]
    psum x1, blocking collectives: 20.9 us -> 12.5 us  [on_device(): low_rank = lax.psum(low, 'tp').astype(jnp.bfloat16)]
  transfers between devices with their start and end apart: 3 -> 9, of which waited for: 2 -> 3; matrix products, arithmetic and copies ran while one was open for 12% -> 52% of each run, Pallas kernels for 0% -> 0%
where the time goes in v1:
time: 157 us; the launch traced here: 155 us
  matrix products  42.5 us (27%)
  local copies, waits for them, and re-layouts  28.6 us (18%)
  other arithmetic  24.4 us (16%)
  between operations  22.8 us (15%)
  waiting for transfers between devices  14.7 us (9%)
  blocking collectives  12.5 us (8%)
  starting transfers between devices  9.58 us (6%)
    dot_general x16, matrix products, term(): low = jnp.dot(own_cols, block[j], preferred_element_type=jnp.float32)  30 us
    psum x1, blocking collectives, on_device(): low_rank = lax.psum(low, 'tp').astype(jnp.bfloat16)  12.5 us
    dot_general x1, local copies, waits for them, and re-layouts, on_device(): jnp.dot(normed, key_value_weight.reshape(model_width, 2 * head_cols), pre...  11.8 us
    ppermute x3, waiting for transfers between devices, on_device(): down_block = lax.ppermute(down_block, 'ad', backward)  11.2 us
    eq x2, other arithmetic, term(): slot_ids == first_id + j  10.1 us
    dot_general x1, matrix products, on_device(): jnp.dot(normed, key_value_weight.reshape(model_width, 2 * head_cols), pre...  9.45 us
    convert_element_type x1, other arithmetic, on_device(): (wide_hidden * inv_rms * gain.astype(jnp.float32)).astype(jnp.bfloat16)  8.73 us
    unnamed x13, local copies, waits for them, and re-layouts  8.05 us
  transfers between devices with their start and end apart: 9, of which 3 were waited for; matrix products, arithmetic and copies ran while one was open for 52% of the time, Pallas kernels for 0%

profile of v1, /device:TPU:0, one launch (start us, length us, event | category | flops | bytes accessed | tf_op | source)
XLA Modules:
  0.0 155.2 jit_solution(1489826976248683410)
XLA Ops:
  6.5 0.0 all-gather.2.cloned.1.call-start
  6.5 3.0 %collective-permute-start.1 = (bf16[2,2048,128]{2,1,0:T(8,128)(2,1)}, bf16[2,2048,128]{2,1,0:T(8,128)(2,1)}, u32[]{:S(2)}, u32[]{:S(2)}) collective-permute-start(bf16[2,2048,128]{2,1,0:T(8,128)(2,1)} %param.12), channel_id=1, source_target_pairs={{2,0},{4,2},{6,4},{7,6},{5,7},{3,5},{1,3},{0,1},{10,8},{12,10},{14... | collective-permute-start | bytes 3145736 | tf_op jit(solution)/shard_map/ppermute | solution.py:62
  9.5 0.1 collective-permute-start
  9.6 0.0 all-gather.2.cloned.1.call-update
  9.6 1.2 dynamic_slice.29
  15.4 0.7 convert_element_type.20
  16.2 4.6 %fusion = f32[448]{0:T(512)S(1)} fusion(bf16[448,8192]{1,0:T(8,128)(2,1)} %param.9), kind=kLoop, calls=%fused_computation.2 | loop fusion | flops 11009600 | bytes 7341824 | tf_op jit(solution)/shard_map/reduce_sum | solution.py:40
  20.8 0.0 copy-done.2
  20.8 0.7 fusion.40
  26.0 0.0 copy-start.1
  26.0 0.0 copy-start.3
  26.0 0.0 copy-start
  26.0 8.7 %fusion.2 = bf16[448,8192]{1,0:T(8,128)(2,1)} fusion(bf16[448,8192]{1,0:T(8,128)(2,1)} %param.9, f32[8192]{0:T(1024)S(1)} %convert_element_type.20, f32[448]{0:T(512)S(1)} %add_rsqrt_fusion), kind=kLoop, calls=%fused_computation.4 | loop fusion | flops 14680064 | bytes 14714624 | tf_op jit(solution)/shard_map/convert_element_type | solution.py:41
  34.8 0.0 copy-done.1
  34.8 0.7 fusion.41
  35.5 0.0 copy-done.3
  35.5 10.1 %broadcast_compare_fusion.1 = (pred[448]{0:T(512)(128)(4,1)S(1)}, s32[448]{0:T(512)S(1)}) fusion(s32[]{:T(128)} %bitcast.46, s32[]{:T(128)} %bitcast.18, s32[]{:T(128)} %bitcast.17, s32[]{:T(128)} %bitcast.16, s32[]{:T(128)} %bitcast.15, s32[]{:T(128)} %bitcast.14, s32[]{:T(128)} %bitcast.13, s32[]{:T(128)} %bitcast.12, s32[]{:T(128)} %bitcast.11, ...), kind=kLoop, calls=%fused_computation.69 | loop fusion | flops 15232 | bytes 4100 | tf_op jit(solution)/shard_map/eq | solution.py:51
  45.6 0.0 copy-done
  45.7 2.2 %convolution_select_fusion.15 = f32[448,128]{1,0:T(8,128)S(1)} fusion(bf16[2,2048,128]{2,1,0:T(8,128)(2,1)S(1)} %copy-done, pred[448]{0:T(512)(128)(4,1)S(1)} %get-tuple-element.26, bf16[448,8192]{1,0:T(8,128)(2,1)} %fusion.2, s32[]{:T(128)S(6)} %select_n.108), kind=kOutput, calls=%fused_computation.41 | convolution fusion | flops 234938368 | bytes 2589188 | tf_op jit(solution)/shard_map/dot_general | solution.py:50
  47.8 2.2 %fusion.25 = f32[448,128]{1,0:T(8,128)S(1)} fusion(f32[448,128]{1,0:T(8,128)S(1)} %convolution_select_fusion.15, bf16[2,2048,128]{2,1,0:T(8,128)(2,1)S(1)} %copy-done, pred[448]{0:T(512)(128)(4,1)S(1)} %get-tuple-element.25, bf16[448,8192]{1,0:T(8,128)(2,1)} %fusion.2, s32[]{:T(128)S(6)} %select_n.108), kind=kOutput, calls=%fused_computation.40 | convolution fusion | flops 234995712 | bytes 2818564 | tf_op jit(solution)/shard_map/dot_general | solution.py:50
  50.0 0.0 collective-permute-done.1
  50.0 2.0 %collective-permute-start.3 = (bf16[2,2048,128]{2,1,0:T(8,128)(2,1)}, bf16[2,2048,128]{2,1,0:T(8,128)(2,1)}, u32[]{:S(2)}, u32[]{:S(2)}) collective-permute-start(bf16[2,2048,128]{2,1,0:T(8,128)(2,1)} %collective-permute-done.1), channel_id=1, source_target_pairs={{2,0},{4,2},{6,4},{7,6},{5,7},{3,5},{1,3},{0,1},{10,8},{12,10},{14... | collective-permute-start | bytes 3145736 | tf_op jit(solution)/shard_map/ppermute | solution.py:62
  52.0 0.0 collective-permute-done
  52.0 0.1 collective-permute-start.2
  52.2 8.0 %copy.20 = bf16[1024,8,2,256]{3,1,2,0:T(8,128)(2,1)} copy(bf16[1024,8,2,256]{3,2,1,0:T(2,128)(2,1)} %bitcast.106) | data formatting | bytes 16777216
  60.2 11.8 %copy.16 = bf16[512,8192]{1,0:T(8,128)(2,1)} copy(bf16[512,8192]{0,1:T(8,128)(2,1)} %bitcast.105) | data formatting | bytes 16777216 | tf_op jit(solution)/shard_map/dot_general | solution.py:70
  72.0 2.2 %convolution_select_fusion.12 = f32[448,128]{1,0:T(8,128)S(1)} fusion(bf16[2,2048,128]{2,1,0:T(8,128)(2,1)} %collective-permute-done, pred[448]{0:T(512)(128)(4,1)S(1)} %get-tuple-element.23, bf16[448,8192]{1,0:T(8,128)(2,1)} %fusion.2, s32[]{:T(128)S(6)} %select_n.108), kind=kOutput, calls=%fused_computation.35 | convolution fusion | flops 234938368 | bytes 2589124 | tf_op jit(solution)/shard_map/dot_general | solution.py:50
  74.3 2.2 %convolution_select_fusion.10 = f32[448,128]{1,0:T(8,128)S(1)} fusion(bf16[2,2048,128]{2,1,0:T(8,128)(2,1)} %collective-permute-done.1, pred[448]{0:T(512)(128)(4,1)S(1)} %get-tuple-element.21, bf16[448,8192]{1,0:T(8,128)(2,1)} %fusion.2, s32[]{:T(128)S(6)} %select_n.108), kind=kOutput, calls=%fused_computation.31 | convolution fusion | flops 234938368 | bytes 2589124 | tf_op jit(solution)/shard_map/dot_general | solution.py:50
  76.5 2.2 %fusion.24 = f32[448,128]{1,0:T(8,128)S(1)} fusion(f32[448,128]{1,0:T(8,128)S(1)} %fusion.25, f32[448,128]{1,0:T(8,128)S(1)} %convolution_select_fusion.12, bf16[2,2048,128]{2,1,0:T(8,128)(2,1)} %collective-permute-done, pred[448]{0:T(512)(128)(4,1)S(1)} %get-tuple-element.24, bf16[448,8192]{1,0:T(8,128)(2,1)} %fusion.2, s32[]{:T(128)S(6)} %select_n.108), kind=kOutput, calls=%fused_computation.38 | convolution fusion | flops 235053056 | bytes 3047876 | tf_op jit(solution)/shard_map/dot_general | solution.py:50
  78.8 0.0 slice-start
  78.8 2.4 %fusion.22 = f32[448,128]{1,0:T(8,128)S(1)} fusion(f32[448,128]{1,0:T(8,128)S(1)} %fusion.24, f32[448,128]{1,0:T(8,128)S(1)} %convolution_select_fusion.10, bf16[2,2048,128]{2,1,0:T(8,128)(2,1)} %collective-permute-done.1, pred[448]{0:T(512)(128)(4,1)S(1)} %get-tuple-element.22, bf16[448,8192]{1,0:T(8,128)(2,1)} %fusion.2, s32[]{:T(128)S(6)} %select_n.108), kind=kOutput, calls=%fused_computation.34 | convolution fusion | flops 235053056 | bytes 3047876 | tf_op jit(solution)/shard_map/dot_general | solution.py:50
  81.2 0.0 collective-permute-done.3
  81.2 2.0 %collective-permute-start.5 = (bf16[2,2048,128]{2,1,0:T(8,128)(2,1)}, bf16[2,2048,128]{2,1,0:T(8,128)(2,1)}, u32[]{:S(2)}, u32[]{:S(2)}) collective-permute-start(bf16[2,2048,128]{2,1,0:T(8,128)(2,1)} %collective-permute-done.3), channel_id=1, source_target_pairs={{2,0},{4,2},{6,4},{7,6},{5,7},{3,5},{1,3},{0,1},{10,8},{12,10},{14... | collective-permute-start | bytes 3145736 | tf_op jit(solution)/shard_map/ppermute | solution.py:62
  83.1 0.0 collective-permute-done.2
  83.1 0.3 collective-permute-start.4
  83.5 2.4 %fusion.38 = (bf16[16,1,64,256]{3,2,1,0:T(8,128)(2,1)}, bf16[16,1,64,256]{3,2,1,0:T(8,128)(2,1)}) fusion(bf16[16,2,64,256]{3,2,1,0:T(8,128)(2,1)} %all-gather.2.cloned.1.call-done), kind=kLoop, calls=%fused_computation.87 | loop fusion | bytes 2097152 | tf_op jit(solution)/shard_map/slice | solution.py:85
  85.9 2.4 %convolution_select_fusion.8 = f32[448,128]{1,0:T(8,128)S(1)} fusion(bf16[2,2048,128]{2,1,0:T(8,128)(2,1)} %collective-permute-done.2, pred[448]{0:T(512)(128)(4,1)S(1)} %get-tuple-element.19, bf16[448,8192]{1,0:T(8,128)(2,1)} %fusion.2, s32[]{:T(128)S(6)} %select_n.108), kind=kOutput, calls=%fused_computation.27 | convolution fusion | flops 234938368 | bytes 2589124 | tf_op jit(solution)/shard_map/dot_general | solution.py:50
  88.3 2.2 %convolution_select_fusion.6 = f32[448,128]{1,0:T(8,128)S(1)} fusion(bf16[2,2048,128]{2,1,0:T(8,128)(2,1)} %collective-permute-done.3, pred[448]{0:T(512)(128)(4,1)S(1)} %get-tuple-element.17, bf16[448,8192]{1,0:T(8,128)(2,1)} %fusion.2, s32[]{:T(128)S(6)} %select_n.108), kind=kOutput, calls=%fused_computation.23 | convolution fusion | flops 234938368 | bytes 2589124 | tf_op jit(solution)/shard_map/dot_general | solution.py:50
  90.5 2.2 %fusion.20 = f32[448,128]{1,0:T(8,128)S(1)} fusion(f32[448,128]{1,0:T(8,128)S(1)} %fusion.22, f32[448,128]{1,0:T(8,128)S(1)} %convolution_select_fusion.8, bf16[2,2048,128]{2,1,0:T(8,128)(2,1)} %collective-permute-done.2, pred[448]{0:T(512)(128)(4,1)S(1)} %get-tuple-element.20, bf16[448,8192]{1,0:T(8,128)(2,1)} %fusion.2, s32[]{:T(128)S(6)} %select_n.108), kind=kOutput, calls=%fused_computation.30 | convolution fusion | flops 235053056 | bytes 3047876 | tf_op jit(solution)/shard_map/dot_general | solution.py:50
  92.8 0.0 slice-done
  92.8 1.7 %fusion.18 = f32[448,128]{1,0:T(8,128)S(1)} fusion(f32[448,128]{1,0:T(8,128)S(1)} %fusion.20, f32[448,128]{1,0:T(8,128)S(1)} %convolution_select_fusion.6, bf16[2,2048,128]{2,1,0:T(8,128)(2,1)} %collective-permute-done.3, pred[448]{0:T(512)(128)(4,1)S(1)} %get-tuple-element.18, bf16[448,8192]{1,0:T(8,128)(2,1)S(1)} %bitcast.104, s32[]{:T(128)S(6)} %select_n.108), kind=kOutput, calls=%fused_computation.26 | convolution fusion | flops 235053056 | bytes 3047940 | tf_op jit(solution)/shard_map/dot_general | solution.py:50
  94.5 11.2 %collective-permute-done.5 = bf16[2,2048,128]{2,1,0:T(8,128)(2,1)} collective-permute-done((bf16[2,2048,128]{2,1,0:T(8,128)(2,1)}, bf16[2,2048,128]{2,1,0:T(8,128)(2,1)}, u32[]{:S(2)}, u32[]{:S(2)}) %collective-permute-start.5) | collective-permute-done | bytes 1048608 | tf_op jit(solution)/shard_map/ppermute | solution.py:62
  105.7 1.1 slice.102
  106.7 1.7 %collective-permute-start.7 = (bf16[1,2048,128]{2,1,0:T(8,128)(2,1)S(1)}, bf16[1,2048,128]{2,1,0:T(8,128)(2,1)S(1)}, u32[]{:S(2)}, u32[]{:S(2)}) collective-permute-start(bf16[1,2048,128]{2,1,0:T(8,128)(2,1)S(1)} %slice.102), channel_id=1, source_target_pairs={{2,0},{4,2},{6,4},{7,6},{5,7},{3,5},{1,3},{0,1},{10,8},{12,10},{14... | collective-permute-start | bytes 1572872 | tf_op jit(solution)/shard_map/ppermute | solution.py:66
  108.4 0.0 collective-permute-done.4
  108.4 1.1 slice.99
  109.5 0.5 collective-permute-start.6
  110.0 1.7 %convolution_select_fusion.4 = f32[448,128]{1,0:T(8,128)S(1)} fusion(bf16[2,2048,128]{2,1,0:T(8,128)(2,1)} %collective-permute-done.4, pred[448]{0:T(512)(128)(4,1)S(1)} %get-tuple-element.15, bf16[448,8192]{1,0:T(8,128)(2,1)S(1)} %bitcast.104, s32[]{:T(128)S(6)} %select_n.108), kind=kOutput, calls=%fused_computation.19 | convolution fusion | flops 234938368 | bytes 2589188 | tf_op jit(solution)/shard_map/dot_general | solution.py:50
  111.6 1.7 %fusion.16 = f32[448,128]{1,0:T(8,128)S(1)} fusion(f32[448,128]{1,0:T(8,128)S(1)} %fusion.18, f32[448,128]{1,0:T(8,128)S(1)} %convolution_select_fusion.4, pred[448]{0:T(512)(128)(4,1)S(1)} %get-tuple-element.16, bf16[2,2048,128]{2,1,0:T(8,128)(2,1)} %collective-permute-done.4, bf16[448,8192]{1,0:T(8,128)(2,1)S(1)} %bitcast.104, s32[]{:T(128)S(6)} %select_n.108), kind=kOutput, calls=%fused_computation.22 | convolution fusion | flops 235053056 | bytes 3047940 | tf_op jit(solution)/shard_map/dot_general | solution.py:50
  113.3 1.7 %convolution_select_fusion.2 = f32[448,128]{1,0:T(8,128)S(1)} fusion(pred[448]{0:T(512)(128)(4,1)S(1)} %get-tuple-element.14, bf16[2,2048,128]{2,1,0:T(8,128)(2,1)} %collective-permute-done.5, bf16[448,8192]{1,0:T(8,128)(2,1)S(1)} %bitcast.104, s32[]{:T(128)S(6)} %select_n.108), kind=kOutput, calls=%fused_computation.15 | convolution fusion | flops 234938368 | bytes 2589188 | tf_op jit(solution)/shard_map/dot_general | solution.py:50
  115.0 1.7 %fusion.14 = f32[448,128]{1,0:T(8,128)S(1)} fusion(f32[448,128]{1,0:T(8,128)S(1)} %fusion.16, f32[448,128]{1,0:T(8,128)S(1)} %convolution_select_fusion.2, bf16[2,2048,128]{2,1,0:T(8,128)(2,1)} %collective-permute-done.5, pred[448]{0:T(512)(128)(4,1)S(1)} %get-tuple-element.13, bf16[448,8192]{1,0:T(8,128)(2,1)S(1)} %bitcast.104, s32[]{:T(128)S(6)} %select_n.108), kind=kOutput, calls=%fused_computation.18 | convolution fusion | flops 235053056 | bytes 3047940 | tf_op jit(solution)/shard_map/dot_general | solution.py:50
  116.7 2.0 %collective-permute-done.7 = bf16[1,2048,128]{2,1,0:T(8,128)(2,1)S(1)} collective-permute-done((bf16[1,2048,128]{2,1,0:T(8,128)(2,1)S(1)}, bf16[1,2048,128]{2,1,0:T(8,128)(2,1)S(1)}, u32[]{:S(2)}, u32[]{:S(2)}) %collective-permute-start.7) | collective-permute-done | bytes 524320 | tf_op jit(solution)/shard_map/ppermute | solution.py:66
  118.8 0.6 convolution_select_fusion
  119.4 1.5 collective-permute-done.6
  120.9 0.6 fusion.12
  121.6 12.5 %all-reduce.1 = bf16[448,128]{1,0:T(8,128)(2,1)S(1)} all-reduce(f32[448,128]{1,0:T(8,128)S(1)} %fusion.12), channel_id=1, replica_groups=mesh['tp'=4,'ad'=8] {'tp'}, use_global_device_ids=true, to_apply=%region_1.2 | all-reduce | flops 57344 | bytes 344064 | tf_op jit(solution)/shard_map/psum | solution.py:69
  134.1 0.1 fusion.39
  134.2 0.1 copy.17
  134.3 0.1 copy.18
  134.4 0.1 broadcast_select_fusion.1
  134.5 1.5 fusion.27
  136.1 1.5 fusion.26
  137.6 9.4 %fusion.8 = bf16[448,2,256]{2,0,1:T(8,128)(2,1)S(1)} fusion(bf16[2,256,8192]{2,1,0:T(8,128)(2,1)} %bitcast.107, bf16[448,8192]{1,0:T(8,128)(2,1)} %fusion.2, bf16[448,1,256]{2,0,1:T(8,128)(2,1)S(1)} %fusion.27, bf16[448,1,256]{2,0,1:T(8,128)(2,1)S(1)} %fusion.26), kind=kOutput, calls=%fused_computation.8 | convolution fusion | flops 3759243264 | bytes 16646144 | tf_op jit(solution)/shard_map/dot_general | solution.py:70
  147.1 1.2 copy.19
  (8 shorter events, 0.1 us)
Async XLA Ops:
  6.5 14.3 %copy-start.2 = (s32[8]{0:T(128)S(1)}, s32[8]{0:T(128)}, u32[]{:S(2)}) copy-start(s32[8]{0:T(128)} %constant.87.clone) | copy-start | bytes 100
  6.5 76.9 %all-gather.2.cloned.1.call-start = ((), (), s32[]{:S(2)}) async-start(), calls=%async_computation | async-start | bytes 1179648 | tf_op jit(solution)/shard_map/all_gather | solution.py:37
  6.5 43.4 %collective-permute-start.1 = (bf16[2,2048,128]{2,1,0:T(8,128)(2,1)}, bf16[2,2048,128]{2,1,0:T(8,128)(2,1)}, u32[]{:S(2)}, u32[]{:S(2)}) collective-permute-start(bf16[2,2048,128]{2,1,0:T(8,128)(2,1)} %param.12), channel_id=1, source_target_pairs={{2,0},{4,2},{6,4},{7,6},{5,7},{3,5},{1,3},{0,1},{10,8},{12,10},{14... | collective-permute-start | bytes 3145736 | tf_op jit(solution)/shard_map/ppermute | solution.py:62
  9.5 42.5 %collective-permute-start = (bf16[2,2048,128]{2,1,0:T(8,128)(2,1)}, bf16[2,2048,128]{2,1,0:T(8,128)(2,1)}, u32[]{:S(2)}, u32[]{:S(2)}) collective-permute-start(bf16[2,2048,128]{2,1,0:T(8,128)(2,1)} %param.12), channel_id=1, source_target_pairs={{0,2},{2,4},{4,6},{6,7},{7,5},{5,3},{3,1},{1,0},{8,10},{10,12},{12... | collective-permute-start | bytes 3145736 | tf_op jit(solution)/shard_map/ppermute | solution.py:61
  26.0 8.8 %copy-start.1 = (s32[16]{0:T(128)S(1)}, s32[16]{0:T(128)}, u32[]{:S(2)}) copy-start(s32[16]{0:T(128)} %param.15) | copy-start | bytes 196
  26.0 9.5 %copy-start.3 = (s32[448]{0:T(512)S(1)}, s32[448]{0:T(512)}, u32[]{:S(2)}) copy-start(s32[448]{0:T(512)} %param.14) | copy-start | bytes 5380
  26.0 19.6 %copy-start = (bf16[2,2048,128]{2,1,0:T(8,128)(2,1)S(1)}, bf16[2,2048,128]{2,1,0:T(8,128)(2,1)}, u32[]{:S(2)}) copy-start(bf16[2,2048,128]{2,1,0:T(8,128)(2,1)} %param.12) | copy-start | bytes 3145732
  50.0 31.2 %collective-permute-start.3 = (bf16[2,2048,128]{2,1,0:T(8,128)(2,1)}, bf16[2,2048,128]{2,1,0:T(8,128)(2,1)}, u32[]{:S(2)}, u32[]{:S(2)}) collective-permute-start(bf16[2,2048,128]{2,1,0:T(8,128)(2,1)} %collective-permute-done.1), channel_id=1, source_target_pairs={{2,0},{4,2},{6,4},{7,6},{5,7},{3,5},{1,3},{0,1},{10,8},{12,10},{14... | collective-permute-start | bytes 3145736 | tf_op jit(solution)/shard_map/ppermute | solution.py:62
  52.0 31.1 %collective-permute-start.2 = (bf16[2,2048,128]{2,1,0:T(8,128)(2,1)}, bf16[2,2048,128]{2,1,0:T(8,128)(2,1)}, u32[]{:S(2)}, u32[]{:S(2)}) collective-permute-start(bf16[2,2048,128]{2,1,0:T(8,128)(2,1)} %collective-permute-done), channel_id=1, source_target_pairs={{0,2},{2,4},{4,6},{6,7},{7,5},{5,3},{3,1},{1,0},{8,10},{10,12},{12... | collective-permute-start | bytes 3145736 | tf_op jit(solution)/shard_map/ppermute | solution.py:61
  78.8 14.0 %slice-start = ((s8[7340032]{0:T(1024)(128)(4,1)}), s8[3145728]{0:T(1024)(128)(4,1)S(1)}, s32[]{:S(2)}) async-start(s8[7340032]{0:T(1024)(128)(4,1)} %bitcast.103), calls=%async_computation.1 | async-start | bytes 6291456
  81.2 24.5 %collective-permute-start.5 = (bf16[2,2048,128]{2,1,0:T(8,128)(2,1)}, bf16[2,2048,128]{2,1,0:T(8,128)(2,1)}, u32[]{:S(2)}, u32[]{:S(2)}) collective-permute-start(bf16[2,2048,128]{2,1,0:T(8,128)(2,1)} %collective-permute-done.3), channel_id=1, source_target_pairs={{2,0},{4,2},{6,4},{7,6},{5,7},{3,5},{1,3},{0,1},{10,8},{12,10},{14... | collective-permute-start | bytes 3145736 | tf_op jit(solution)/shard_map/ppermute | solution.py:62
  83.1 25.3 %collective-permute-start.4 = (bf16[2,2048,128]{2,1,0:T(8,128)(2,1)}, bf16[2,2048,128]{2,1,0:T(8,128)(2,1)}, u32[]{:S(2)}, u32[]{:S(2)}) collective-permute-start(bf16[2,2048,128]{2,1,0:T(8,128)(2,1)} %collective-permute-done.2), channel_id=1, source_target_pairs={{0,2},{2,4},{4,6},{6,7},{7,5},{5,3},{3,1},{1,0},{8,10},{10,12},{12... | collective-permute-start | bytes 3145736 | tf_op jit(solution)/shard_map/ppermute | solution.py:61
  85.9 6.9 %slice-start.1 = ((s8[7340032]{0:T(1024)(128)(4,1)}), s8[4194304]{0:T(1024)(128)(4,1)S(1)}, s32[]{:S(2)}) async-start(s8[7340032]{0:T(1024)(128)(4,1)} %bitcast.103), calls=%async_computation.2 | async-start | bytes 8388608
  106.7 12.0 %collective-permute-start.7 = (bf16[1,2048,128]{2,1,0:T(8,128)(2,1)S(1)}, bf16[1,2048,128]{2,1,0:T(8,128)(2,1)S(1)}, u32[]{:S(2)}, u32[]{:S(2)}) collective-permute-start(bf16[1,2048,128]{2,1,0:T(8,128)(2,1)S(1)} %slice.102), channel_id=1, source_target_pairs={{2,0},{4,2},{6,4},{7,6},{5,7},{3,5},{1,3},{0,1},{10,8},{12,10},{14... | collective-permute-start | bytes 1572872 | tf_op jit(solution)/shard_map/ppermute | solution.py:66
  109.5 11.4 %collective-permute-start.6 = (bf16[1,2048,128]{2,1,0:T(8,128)(2,1)S(1)}, bf16[1,2048,128]{2,1,0:T(8,128)(2,1)S(1)}, u32[]{:S(2)}, u32[]{:S(2)}) collective-permute-start(bf16[1,2048,128]{2,1,0:T(8,128)(2,1)S(1)} %slice.99), channel_id=1, source_target_pairs={{0,2},{2,4},{4,6},{6,7},{7,5},{5,3},{3,1},{1,0},{8,10},{10,12},{12... | collective-permute-start | bytes 1572872 | tf_op jit(solution)/shard_map/ppermute | solution.py:65
Sparse Core Ops, SparseCore 0:
  9.7 44.8 all-gather.1

commit v2 on v1

--- a/solution.py
+++ b/solution.py
@@ -9,6 +9,14 @@
 
 def ring_order(count):
     return list(range(0, count, 2)) + list(reversed(range(1, count, 2)))
+
+
+def tie(*values):
+    return lax.optimization_barrier(values)
+
+
+def base_of(normed, *parts):
+    return [jnp.dot(normed, part, preferred_element_type=jnp.float32) for part in parts]
 
 
 def on_device(
@@ -36,45 +44,70 @@
 
     up_all = lax.all_gather(adapter_up_weight, "ad", axis=0, tiled=True)
 
+    pairs = jnp.arange(adapter_row_index.shape[0], dtype=jnp.int32)
+    is_pair = language_pair_index[:, None] == pairs[None, :]
+    slot_ids = jnp.sum(jnp.where(is_pair, adapter_row_index[None, :], 0), axis=1, keepdims=True)
+
     wide_hidden = hidden.astype(jnp.float32)
     inv_rms = lax.rsqrt(jnp.mean(wide_hidden * wide_hidden, axis=-1, keepdims=True) + epsilon)
     normed = (wide_hidden * inv_rms * gain.astype(jnp.float32)).astype(jnp.bfloat16)
     own_cols = lax.dynamic_slice_in_dim(
         normed, lax.axis_index("tp") * column_portion, column_portion, 1
     )
-    slot_ids = adapter_row_index[language_pair_index]
+    own_cols, normed, slot_ids = tie(own_cols, normed, slot_ids)
 
     def term(block, first_id):
-        total = jnp.zeros((tok_count, low_width), jnp.float32)
+        total = jnp.float32(0.0)
         for j in range(block.shape[0]):
             low = jnp.dot(own_cols, block[j], preferred_element_type=jnp.float32)
-            total = total + jnp.where((slot_ids == first_id + j)[:, None], low, jnp.float32(0.0))
+            total = total + jnp.where(slot_ids == first_id + j, low, jnp.float32(0.0))
         return total
 
+    steps = owners // 2
+    half = held // 2
+    up_block = down_block = adapter_down_weight
     low = term(adapter_down_weight, me * held)
-    up_block = down_block = adapter_down_weight
-    half = held // 2
-    for step in range(1, owners // 2 + 1):
+    waiting = []
+    for step in range(1, steps + 1):
         from_behind = order_table[lax.rem(my_place + owners - step, owners)]
         from_ahead = order_table[lax.rem(my_place + step, owners)]
-        if step < owners // 2:
-            up_block = lax.ppermute(up_block, "ad", forward)
-            down_block = lax.ppermute(down_block, "ad", backward)
-            low = low + term(up_block, from_behind * held) + term(down_block, from_ahead * held)
+        if step == steps:
+            up_block, down_block = up_block[:half], down_block[half:]
+        up_next = lax.ppermute(up_block, "ad", forward)
+        down_next = lax.ppermute(down_block, "ad", backward)
+        if step == 2:
+            key_value_weight, up_block, down_block = tie(key_value_weight, up_block, down_block)
+            key_part, value_part = tie(key_value_weight[:, 0], key_value_weight[:, 1])
+        if step == 3:
+            key_part, value_part, up_block, down_block = tie(
+                key_part, value_part, up_block, down_block
+            )
+            base = base_of(normed, key_part, value_part)
+        if step >= 3:
+            for block, owner in waiting:
+                low = low + term(block, owner * held)
+            waiting = []
+        if step < steps:
+            if step == 1:
+                up_next, down_next, low = tie(up_next, down_next, low)
+            elif step == 2:
+                up_next, down_next, key_part, value_part = tie(
+                    up_next, down_next, key_part, value_part
+                )
+            elif step == 3:
+                up_next, down_next, low, *base = tie(up_next, down_next, low, *base)
+            else:
+                up_next, down_next, low = tie(up_next, down_next, low)
+            waiting += [(up_next, from_behind), (down_next, from_ahead)]
         else:
-            first = lax.ppermute(up_block[:half], "ad", forward)
-            rest = lax.ppermute(down_block[half:], "ad", backward)
-            low = low + term(first, from_behind * held) + term(rest, from_ahead * held + half)
+            low = low + term(up_next, from_behind * held)
+            low = low + term(down_next, from_ahead * held + half)
+        up_block, down_block = up_next, down_next
 
     low_rank = lax.psum(low, "tp").astype(jnp.bfloat16)
-    base = jnp.dot(
-        normed,
-        key_value_weight.reshape(model_width, 2 * head_cols),
-        preferred_element_type=jnp.float32,
-    ).reshape(tok_count, 2, head_cols)
 
     adapters = up_all.shape[0]
-    mask = slot_ids[:, None] == jnp.arange(adapters, dtype=jnp.int32)[None, :]
+    mask = slot_ids == jnp.arange(adapters, dtype=jnp.int32)[None, :]
     halves = []
     for c in range(2):
         part = low_rank[:, c * rank : (c + 1) * rank]
@@ -86,8 +119,11 @@
                 preferred_element_type=jnp.float32,
             )
         )
-    delta = jnp.stack(halves, axis=1).astype(jnp.bfloat16)
-    return (base + adapter_scale * delta.astype(jnp.float32)).astype(jnp.bfloat16)
+    outs = [
+        (part + adapter_scale * delta.astype(jnp.bfloat16).astype(jnp.float32)).astype(jnp.bfloat16)
+        for part, delta in zip(base, halves)
+    ]
+    return jnp.stack(outs, axis=1)
 
 
 def solution(mesh):

time: 157 us -> 135 us (0.86)
  matrix products: 42.5 us -> 27.4 us
  waiting for transfers between devices: 14.7 us -> 28.6 us
  other arithmetic: 24.4 us -> 11.4 us
  local copies, waits for them, and re-layouts: 28.6 us -> 22.1 us
    ppermute x8, waiting for transfers between devices: 14.7 us -> 28.6 us  [the longest x4 23.1 us: on_device(): up_next = lax.ppermute(up_block, 'ad', forward)]
    dot_general x1 -> x0, local copies, waits for them, and re-layouts: 11.8 us -> none  [on_device(): jnp.dot(normed, key_value_weight.reshape(model_width, 2 * head_cols), pre...]
    dot_general x16, matrix products: 30 us -> 19.1 us  [term(): low = jnp.dot(own_cols, block[j], preferred_element_type=jnp.float32)]
    eq x3 -> x2, other arithmetic: 10.1 us -> 0.14 us  [the longest x1 0.13 us: term(): total = total + jnp.where(slot_ids == first_id + j, low, jnp.float32(0.0))]
    optimization_barrier x0 -> x1, local copies, waits for them, and re-layouts: none -> 7.69 us  [tie(): return lax.optimization_barrier(values)]
    squeeze x0 -> x1, local copies, waits for them, and re-layouts: none -> 5.79 us  [on_device(): key_part, value_part = tie(key_value_weight[:, 0], key_value_weight[:, 1])]
    unnamed x13 -> x22, local copies, waits for them, and re-layouts: 8.05 us -> 3.53 us
    convert_element_type x1, other arithmetic: 8.73 us -> 5.5 us  [on_device(): (wide_hidden * inv_rms * gain.astype(jnp.float32)).astype(jnp.bfloat16)]
  transfers between devices with their start and end apart: 9 -> 9, of which waited for: 3 -> 8; matrix products, arithmetic and copies ran while one was open for 52% -> 40% of each run, Pallas kernels for 0% -> 0%
where the time goes in v2:
time: 135 us; the launch traced here: 134 us
  waiting for transfers between devices  28.6 us (21%)
  matrix products  27.4 us (20%)
  between operations  22.8 us (17%)
  local copies, waits for them, and re-layouts  22.1 us (16%)
  blocking collectives  12.6 us (9%)
  other arithmetic  11.4 us (8%)
  starting transfers between devices  9.21 us (7%)
    ppermute x4, waiting for transfers between devices, on_device(): up_next = lax.ppermute(up_block, 'ad', forward)  23.1 us
    dot_general x16, matrix products, term(): low = jnp.dot(own_cols, block[j], preferred_element_type=jnp.float32)  19.1 us
    psum x1, blocking collectives, on_device(): low_rank = lax.psum(low, 'tp').astype(jnp.bfloat16)  12.6 us
    optimization_barrier x1, local copies, waits for them, and re-layouts, tie(): return lax.optimization_barrier(values)  7.69 us
    dot_general x2, matrix products, base_of(): jnp.dot(normed, part, preferred_element_type=jnp.float32)  7.39 us
    ppermute x4, starting transfers between devices, on_device(): up_next = lax.ppermute(up_block, 'ad', forward)  7.25 us
    squeeze x1, local copies, waits for them, and re-layouts, on_device(): key_part, value_part = tie(key_value_weight[:, 0], key_value_weight[:, 1])  5.79 us
    convert_element_type x1, other arithmetic, on_device(): (wide_hidden * inv_rms * gain.astype(jnp.float32)).astype(jnp.bfloat16)  5.5 us
  transfers between devices with their start and end apart: 9, of which 8 were waited for; matrix products, arithmetic and copies ran while one was open for 40% of the time, Pallas kernels for 0%

profile of v2, /device:TPU:0, one launch (start us, length us, event | category | flops | bytes accessed | tf_op | source)
XLA Modules:
  0.0 134.1 jit_solution(3117990357732223896)
XLA Ops:
  6.5 0.0 all-gather.2.cloned.1.call-start
  6.5 3.0 %collective-permute-start = (bf16[2,2048,128]{2,1,0:T(8,128)(2,1)}, bf16[2,2048,128]{2,1,0:T(8,128)(2,1)}, u32[]{:S(2)}, u32[]{:S(2)}) collective-permute-start(bf16[2,2048,128]{2,1,0:T(8,128)(2,1)} %param.12), channel_id=1, source_target_pairs={{0,2},{2,4},{4,6},{6,7},{7,5},{5,3},{3,1},{1,0},{8,10},{10,12},{12... | collective-permute-start | bytes 3145736 | tf_op jit(solution)/shard_map/ppermute | solution.py:76
  9.6 0.0 collective-permute-start.1
  9.6 0.0 all-gather.2.cloned.1.call-update
  9.6 0.7 convert_element_type.31
  10.3 4.6 %fusion = f32[448]{0:T(512)S(1)} fusion(bf16[448,8192]{1,0:T(8,128)(2,1)} %param.9), kind=kLoop, calls=%fused_computation.2 | loop fusion | flops 11009600 | bytes 7341824 | tf_op jit(solution)/shard_map/reduce_sum | solution.py:52
  14.9 5.5 %fusion.2 = bf16[448,8192]{1,0:T(8,128)(2,1)S(1)} fusion(bf16[448,8192]{1,0:T(8,128)(2,1)} %param.9, f32[8192]{0:T(1024)S(1)} %convert_element_type.31, f32[448]{0:T(512)S(1)} %add_rsqrt_fusion), kind=kLoop, calls=%fused_computation.4 | loop fusion | flops 14680064 | bytes 14714624 | tf_op jit(solution)/shard_map/convert_element_type | solution.py:53
  20.4 3.0 %copy-done = bf16[448,8192]{1,0:T(8,128)(2,1)} copy-done((bf16[448,8192]{1,0:T(8,128)(2,1)}, bf16[448,8192]{1,0:T(8,128)(2,1)S(1)}, u32[]{:S(2)}) %copy-start) | copy-done | bytes 7340056
  23.5 0.0 copy-start.4
  23.5 0.1 constant_dynamic-slice_fusion
  23.6 0.5 copy-done.8
  24.1 0.6 dynamic_slice.29
  29.3 0.0 copy-done.5
  29.3 0.7 fusion.51
  34.4 0.1 select_reduce_fusion
  34.5 0.1 compare_reduce_fusion
  34.7 0.6 convolution_select_fusion.15
  35.3 0.6 fusion.14
  36.0 0.6 collective-permute-done
  36.5 2.2 %collective-permute-done.1 = bf16[2,2048,128]{2,1,0:T(8,128)(2,1)} collective-permute-done((bf16[2,2048,128]{2,1,0:T(8,128)(2,1)}, bf16[2,2048,128]{2,1,0:T(8,128)(2,1)}, u32[]{:S(2)}, u32[]{:S(2)}) %collective-permute-start.1) | collective-permute-done | bytes 1048608 | tf_op jit(solution)/shard_map/ppermute | solution.py:77
  38.7 1.6 %collective-permute-start.2 = (bf16[2,2048,128]{2,1,0:T(8,128)(2,1)}, bf16[2,2048,128]{2,1,0:T(8,128)(2,1)}, u32[]{:S(2)}, u32[]{:S(2)}) collective-permute-start(bf16[2,2048,128]{2,1,0:T(8,128)(2,1)} %collective-permute-done), channel_id=1, source_target_pairs={{0,2},{2,4},{4,6},{6,7},{7,5},{5,3},{3,1},{1,0},{8,10},{10,12},{12... | collective-permute-start | bytes 3145736 | tf_op jit(solution)/shard_map/ppermute | solution.py:76
  40.3 0.4 collective-permute-start.3
  40.7 7.7 %copy.21 = bf16[8192,2,256]{2,0,1:T(8,128)(2,1)} copy(bf16[8192,2,256]{2,1,0:T(2,128)(2,1)} %param.11) | data formatting | bytes 16777216 | tf_op jit(solution)/shard_map/optimization_barrier | solution.py:15
  48.4 5.8 %slice_bitcast_fusion = (bf16[8192,256]{1,0:T(8,128)(2,1)}, bf16[8192,256]{1,0:T(8,128)(2,1)}) fusion(bf16[8192,2,256]{2,0,1:T(8,128)(2,1)} %copy.21), kind=kLoop, calls=%fused_computation.5 | loop fusion | bytes 16777216 | tf_op jit(solution)/shard_map/squeeze | solution.py:80
  54.2 1.7 %convolution_select_fusion.13 = f32[448,128]{1,0:T(8,128)S(1)} fusion(bf16[448,2048]{1,0:T(8,128)(2,1)S(1)} %constant_dynamic-slice_fusion, bf16[2,2048,128]{2,1,0:T(8,128)(2,1)} %collective-permute-done, pred[448]{0:T(512)(128)(4,1)S(1)} %get-tuple-element.58), kind=kOutput, calls=%fused_computation.33 | convolution fusion | flops 234938368 | bytes 2589120 | tf_op jit(solution)/shard_map/dot_general | solution.py:62
  55.9 1.7 %convolution_select_fusion.11 = f32[448,128]{1,0:T(8,128)S(1)} fusion(bf16[448,2048]{1,0:T(8,128)(2,1)S(1)} %constant_dynamic-slice_fusion, bf16[2,2048,128]{2,1,0:T(8,128)(2,1)} %collective-permute-done.1, pred[448]{0:T(512)(128)(4,1)S(1)} %get-tuple-element.56), kind=kOutput, calls=%fused_computation.30 | convolution fusion | flops 234938368 | bytes 2589120 | tf_op jit(solution)/shard_map/dot_general | solution.py:62
  57.6 1.7 %fusion.13 = f32[448,128]{1,0:T(8,128)S(1)} fusion(f32[448,128]{1,0:T(8,128)S(1)} %convolution_select_fusion.13, bf16[448,2048]{1,0:T(8,128)(2,1)S(1)} %constant_dynamic-slice_fusion, bf16[2,2048,128]{2,1,0:T(8,128)(2,1)} %collective-permute-done, pred[448]{0:T(512)(128)(4,1)S(1)} %get-tuple-element.57), kind=kOutput, calls=%fused_computation.32 | convolution fusion | flops 234995712 | bytes 2818496 | tf_op jit(solution)/shard_map/dot_general | solution.py:62
  59.3 1.7 %fusion.12 = f32[448,128]{1,0:T(8,128)S(1)} fusion(f32[448,128]{1,0:T(8,128)S(1)} %convolution_select_fusion.11, bf16[448,2048]{1,0:T(8,128)(2,1)S(1)} %constant_dynamic-slice_fusion, bf16[2,2048,128]{2,1,0:T(8,128)(2,1)} %collective-permute-done.1, pred[448]{0:T(512)(128)(4,1)S(1)} %get-tuple-element.55), kind=kOutput, calls=%fused_computation.29 | convolution fusion | flops 234995712 | bytes 2818496 | tf_op jit(solution)/shard_map/dot_general | solution.py:62
  61.0 0.0 all-gather.2.cloned.1.call-done
  61.0 2.1 %fusion.49 = (bf16[16,1,64,256]{3,2,1,0:T(8,128)(2,1)S(1)}, bf16[16,1,64,256]{3,2,1,0:T(8,128)(2,1)}) fusion(bf16[16,2,64,256]{3,2,1,0:T(8,128)(2,1)} %all-gather.2.cloned.1.call-done), kind=kLoop, calls=%fused_computation.96 | loop fusion | bytes 2097152 | tf_op jit(solution)/shard_map/slice | solution.py:118
  63.1 6.8 %collective-permute-done.2 = bf16[2,2048,128]{2,1,0:T(8,128)(2,1)} collective-permute-done((bf16[2,2048,128]{2,1,0:T(8,128)(2,1)}, bf16[2,2048,128]{2,1,0:T(8,128)(2,1)}, u32[]{:S(2)}, u32[]{:S(2)}) %collective-permute-start.2) | collective-permute-done | bytes 1048608 | tf_op jit(solution)/shard_map/ppermute | solution.py:76
  69.9 2.2 %collective-permute-done.3 = bf16[2,2048,128]{2,1,0:T(8,128)(2,1)} collective-permute-done((bf16[2,2048,128]{2,1,0:T(8,128)(2,1)}, bf16[2,2048,128]{2,1,0:T(8,128)(2,1)}, u32[]{:S(2)}, u32[]{:S(2)}) %collective-permute-start.3) | collective-permute-done | bytes 1048608 | tf_op jit(solution)/shard_map/ppermute | solution.py:77
  72.1 1.5 %collective-permute-start.4 = (bf16[2,2048,128]{2,1,0:T(8,128)(2,1)}, bf16[2,2048,128]{2,1,0:T(8,128)(2,1)S(1)}, u32[]{:S(2)}, u32[]{:S(2)}) collective-permute-start(bf16[2,2048,128]{2,1,0:T(8,128)(2,1)} %collective-permute-done.2), channel_id=1, source_target_pairs={{0,2},{2,4},{4,6},{6,7},{7,5},{5,3},{3,1},{1,0},{8,10},{10,12},{12... | collective-permute-start | bytes 3145736 | tf_op jit(solution)/shard_map/ppermute | solution.py:76
  73.6 0.5 collective-permute-start.5
  74.1 1.8 %convolution_select_fusion.9 = f32[448,128]{1,0:T(8,128)S(1)} fusion(bf16[448,2048]{1,0:T(8,128)(2,1)S(1)} %constant_dynamic-slice_fusion, bf16[2,2048,128]{2,1,0:T(8,128)(2,1)} %collective-permute-done.2, pred[448]{0:T(512)(128)(4,1)S(1)} %get-tuple-element.54), kind=kOutput, calls=%fused_computation.27 | convolution fusion | flops 234938368 | bytes 2589120 | tf_op jit(solution)/shard_map/dot_general | solution.py:62
  75.9 0.0 slice-start
  75.9 1.8 %convolution_select_fusion.7 = f32[448,128]{1,0:T(8,128)S(1)} fusion(bf16[448,2048]{1,0:T(8,128)(2,1)S(1)} %constant_dynamic-slice_fusion, bf16[2,2048,128]{2,1,0:T(8,128)(2,1)} %collective-permute-done.3, pred[448]{0:T(512)(128)(4,1)S(1)} %get-tuple-element.52), kind=kOutput, calls=%fused_computation.24 | convolution fusion | flops 234938368 | bytes 2589120 | tf_op jit(solution)/shard_map/dot_general | solution.py:62
  77.8 0.0 copy-done.2
  77.8 0.0 slice-start.1
  77.8 5.3 %fusion.53 = f32[448,256]{1,0:T(8,128)S(1)} fusion(bf16[448,8192]{1,0:T(8,128)(2,1)} %copy-done, bf16[8192,256]{1,0:T(8,128)(2,1)S(1)} %copy-done.2), kind=kOutput, calls=%fused_computation.100 | convolution fusion | flops 1879048192 | bytes 11993088 | tf_op jit(solution)/shard_map/dot_general | solution.py:19
  83.2 1.8 %fusion.11 = f32[448,128]{1,0:T(8,128)S(1)} fusion(f32[448,128]{1,0:T(8,128)S(1)} %convolution_select_fusion.9, bf16[448,2048]{1,0:T(8,128)(2,1)S(1)} %constant_dynamic-slice_fusion, bf16[2,2048,128]{2,1,0:T(8,128)(2,1)} %collective-permute-done.2, pred[448]{0:T(512)(128)(4,1)S(1)} %get-tuple-element.53), kind=kOutput, calls=%fused_computation.26 | convolution fusion | flops 234995712 | bytes 2818496 | tf_op jit(solution)/shard_map/dot_general | solution.py:62
  85.0 1.7 %fusion.10 = f32[448,128]{1,0:T(8,128)S(1)} fusion(f32[448,128]{1,0:T(8,128)S(1)} %convolution_select_fusion.7, bf16[448,2048]{1,0:T(8,128)(2,1)S(1)} %constant_dynamic-slice_fusion, bf16[2,2048,128]{2,1,0:T(8,128)(2,1)} %collective-permute-done.3, f32[448,128]{1,0:T(8,128)S(1)} %fusion.11, f32[448,128]{1,0:T(8,128)S(1)} %fusion.12, ...), kind=kOutput, calls=%fused_computation.23 | convolution fusion | flops 235225088 | bytes 3736000 | tf_op jit(solution)/shard_map/dot_general | solution.py:62
  86.7 2.1 %fusion.52 = f32[448,256]{1,0:T(8,128)S(1)} fusion(bf16[448,8192]{1,0:T(8,128)(2,1)S(1)} %bitcast.103, bf16[8192,256]{1,0:T(8,128)(2,1)S(1)} %copy-done.1), kind=kOutput, calls=%fused_computation.99 | convolution fusion | flops 1879048192 | bytes 11993088 | tf_op jit(solution)/shard_map/dot_general | solution.py:19
  88.8 8.1 %collective-permute-done.4 = bf16[2,2048,128]{2,1,0:T(8,128)(2,1)S(1)} collective-permute-done((bf16[2,2048,128]{2,1,0:T(8,128)(2,1)}, bf16[2,2048,128]{2,1,0:T(8,128)(2,1)S(1)}, u32[]{:S(2)}, u32[]{:S(2)}) %collective-permute-start.4) | collective-permute-done | bytes 1048608 | tf_op jit(solution)/shard_map/ppermute | solution.py:76
  96.9 0.8 collective-permute-done.5
  97.7 0.6 convolution_select_fusion.5
  98.4 1.2 collective-permute-start.6
  99.6 1.0 collective-permute-start.7
  100.5 0.6 fusion.8
  101.2 0.6 convolution_select_fusion.3
  101.8 0.6 fusion.7
  102.5 7.7 %collective-permute-done.6 = bf16[1,2048,128]{2,1,0:T(8,128)(2,1)S(1)} collective-permute-done((bf16[1,2048,128]{2,1,0:T(8,128)(2,1)S(1)}, bf16[1,2048,128]{2,1,0:T(8,128)(2,1)S(1)}, u32[]{:S(2)}, u32[]{:S(2)}) %collective-permute-start.6) | collective-permute-done | bytes 524320 | tf_op jit(solution)/shard_map/ppermute | solution.py:76
  110.2 0.6 convolution_select_fusion.1
  110.8 0.3 collective-permute-done.7
  111.1 0.6 add_add_fusion
  111.8 12.6 %all-reduce.1 = bf16[448,128]{1,0:T(8,128)(2,1)S(1)} all-reduce(f32[448,128]{1,0:T(8,128)S(1)} %add_add_fusion), channel_id=1, replica_groups=mesh['tp'=4,'ad'=8] {'tp'}, use_global_device_ids=true, to_apply=%region_2.3 | all-reduce | flops 57344 | bytes 344064 | tf_op jit(solution)/shard_map/psum | solution.py:107
  124.4 0.1 fusion.50
  124.5 0.1 copy.23
  124.6 0.1 copy.24
  124.7 0.1 broadcast_select_fusion.1
  124.9 0.5 fusion.4
  125.3 0.5 fusion.6
  125.8 0.1 fusion.43
  126.0 1.2 copy.25
  (21 shorter events, 0.2 us)
Async XLA Ops:
  6.5 54.5 %all-gather.2.cloned.1.call-start = ((), (), s32[]{:S(2)}) async-start(), calls=%async_computation | async-start | bytes 1179648 | tf_op jit(solution)/shard_map/all_gather | solution.py:45
  6.5 30.0 %collective-permute-start = (bf16[2,2048,128]{2,1,0:T(8,128)(2,1)}, bf16[2,2048,128]{2,1,0:T(8,128)(2,1)}, u32[]{:S(2)}, u32[]{:S(2)}) collective-permute-start(bf16[2,2048,128]{2,1,0:T(8,128)(2,1)} %param.12), channel_id=1, source_target_pairs={{0,2},{2,4},{4,6},{6,7},{7,5},{5,3},{3,1},{1,0},{8,10},{10,12},{12... | collective-permute-start | bytes 3145736 | tf_op jit(solution)/shard_map/ppermute | solution.py:76
  9.6 29.1 %collective-permute-start.1 = (bf16[2,2048,128]{2,1,0:T(8,128)(2,1)}, bf16[2,2048,128]{2,1,0:T(8,128)(2,1)}, u32[]{:S(2)}, u32[]{:S(2)}) collective-permute-start(bf16[2,2048,128]{2,1,0:T(8,128)(2,1)} %param.12), channel_id=1, source_target_pairs={{2,0},{4,2},{6,4},{7,6},{5,7},{3,5},{1,3},{0,1},{10,8},{12,10},{14... | collective-permute-start | bytes 3145736 | tf_op jit(solution)/shard_map/ppermute | solution.py:77
  20.4 3.0 %copy-start = (bf16[448,8192]{1,0:T(8,128)(2,1)}, bf16[448,8192]{1,0:T(8,128)(2,1)S(1)}, u32[]{:S(2)}) copy-start(bf16[448,8192]{1,0:T(8,128)(2,1)S(1)} %fusion.2) | copy-start | bytes 22020100
  23.4 0.7 copy-start.8
  23.4 5.8 %copy-start.5 = (s32[8]{0:T(128)S(1)}, s32[8]{0:T(128)}, u32[]{:S(2)}) copy-start(s32[8]{0:T(128)} %constant.84.clone) | copy-start | bytes 100
  23.4 10.9 %copy-start.6 = (s32[448]{0:T(512)S(1)}, s32[448]{0:T(512)}, u32[]{:S(2)}) copy-start(s32[448]{0:T(512)} %param.14) | copy-start | bytes 5380
  23.4 11.0 %copy-start.7 = (s32[16]{0:T(128)S(1)}, s32[16]{0:T(128)}, u32[]{:S(2)}) copy-start(s32[16]{0:T(128)} %param.15) | copy-start | bytes 196
  23.5 11.2 %copy-start.4 = (bf16[2,2048,128]{2,1,0:T(8,128)(2,1)S(1)}, bf16[2,2048,128]{2,1,0:T(8,128)(2,1)}, u32[]{:S(2)}) copy-start(bf16[2,2048,128]{2,1,0:T(8,128)(2,1)} %param.12) | copy-start | bytes 3145732
  38.7 31.2 %collective-permute-start.2 = (bf16[2,2048,128]{2,1,0:T(8,128)(2,1)}, bf16[2,2048,128]{2,1,0:T(8,128)(2,1)}, u32[]{:S(2)}, u32[]{:S(2)}) collective-permute-start(bf16[2,2048,128]{2,1,0:T(8,128)(2,1)} %collective-permute-done), channel_id=1, source_target_pairs={{0,2},{2,4},{4,6},{6,7},{7,5},{5,3},{3,1},{1,0},{8,10},{10,12},{12... | collective-permute-start | bytes 3145736 | tf_op jit(solution)/shard_map/ppermute | solution.py:76
  40.3 31.8 %collective-permute-start.3 = (bf16[2,2048,128]{2,1,0:T(8,128)(2,1)}, bf16[2,2048,128]{2,1,0:T(8,128)(2,1)}, u32[]{:S(2)}, u32[]{:S(2)}) collective-permute-start(bf16[2,2048,128]{2,1,0:T(8,128)(2,1)} %collective-permute-done.1), channel_id=1, source_target_pairs={{2,0},{4,2},{6,4},{7,6},{5,7},{3,5},{1,3},{0,1},{10,8},{12,10},{14... | collective-permute-start | bytes 3145736 | tf_op jit(solution)/shard_map/ppermute | solution.py:77
  72.1 24.8 %collective-permute-start.4 = (bf16[2,2048,128]{2,1,0:T(8,128)(2,1)}, bf16[2,2048,128]{2,1,0:T(8,128)(2,1)S(1)}, u32[]{:S(2)}, u32[]{:S(2)}) collective-permute-start(bf16[2,2048,128]{2,1,0:T(8,128)(2,1)} %collective-permute-done.2), channel_id=1, source_target_pairs={{0,2},{2,4},{4,6},{6,7},{7,5},{5,3},{3,1},{1,0},{8,10},{10,12},{12... | collective-permute-start | bytes 3145736 | tf_op jit(solution)/shard_map/ppermute | solution.py:76
  73.6 24.1 %collective-permute-start.5 = (bf16[2,2048,128]{2,1,0:T(8,128)(2,1)}, bf16[2,2048,128]{2,1,0:T(8,128)(2,1)S(1)}, u32[]{:S(2)}, u32[]{:S(2)}) collective-permute-start(bf16[2,2048,128]{2,1,0:T(8,128)(2,1)} %collective-permute-done.3), channel_id=1, source_target_pairs={{2,0},{4,2},{6,4},{7,6},{5,7},{3,5},{1,3},{0,1},{10,8},{12,10},{14... | collective-permute-start | bytes 3145736 | tf_op jit(solution)/shard_map/ppermute | solution.py:77
  74.1 3.7 %copy-start.2 = (bf16[8192,256]{1,0:T(8,128)(2,1)S(1)}, bf16[8192,256]{1,0:T(8,128)(2,1)}, u32[]{:S(2)}) copy-start(bf16[8192,256]{1,0:T(8,128)(2,1)} %get-tuple-element.39) | copy-start | bytes 12582916
  75.9 10.8 %slice-start = ((s8[7340032]{0:T(1024)(128)(4,1)}), s8[4194304]{0:T(1024)(128)(4,1)S(1)}, s32[]{:S(2)}) async-start(s8[7340032]{0:T(1024)(128)(4,1)} %bitcast.102), calls=%async_computation.1 | async-start | bytes 8388608
  77.8 8.9 %slice-start.1 = ((s8[7340032]{0:T(1024)(128)(4,1)}), s8[3145728]{0:T(1024)(128)(4,1)S(1)}, s32[]{:S(2)}) async-start(s8[7340032]{0:T(1024)(128)(4,1)} %bitcast.102), calls=%async_computation.2 | async-start | bytes 6291456
  83.1 3.6 %copy-start.1 = (bf16[8192,256]{1,0:T(8,128)(2,1)S(1)}, bf16[8192,256]{1,0:T(8,128)(2,1)}, u32[]{:S(2)}) copy-start(bf16[8192,256]{1,0:T(8,128)(2,1)} %get-tuple-element.38) | copy-start | bytes 12582916
  98.4 11.8 %collective-permute-start.6 = (bf16[1,2048,128]{2,1,0:T(8,128)(2,1)S(1)}, bf16[1,2048,128]{2,1,0:T(8,128)(2,1)S(1)}, u32[]{:S(2)}, u32[]{:S(2)}) collective-permute-start(bf16[1,2048,128]{2,1,0:T(8,128)(2,1)S(1)} %slice.74), channel_id=1, source_target_pairs={{0,2},{2,4},{4,6},{6,7},{7,5},{5,3},{3,1},{1,0},{8,10},{10,12},{12... | collective-permute-start | bytes 1572872 | tf_op jit(solution)/shard_map/ppermute | solution.py:76
  99.6 11.6 %collective-permute-start.7 = (bf16[1,2048,128]{2,1,0:T(8,128)(2,1)S(1)}, bf16[1,2048,128]{2,1,0:T(8,128)(2,1)S(1)}, u32[]{:S(2)}, u32[]{:S(2)}) collective-permute-start(bf16[1,2048,128]{2,1,0:T(8,128)(2,1)S(1)} %slice.77), channel_id=1, source_target_pairs={{2,0},{4,2},{6,4},{7,6},{5,7},{3,5},{1,3},{0,1},{10,8},{12,10},{14... | collective-permute-start | bytes 1572872 | tf_op jit(solution)/shard_map/ppermute | solution.py:77
  111.8 13.1 %copy-start.3 = (bf16[16,1,64,256]{3,2,1,0:T(8,128)(2,1)S(1)}, bf16[16,1,64,256]{3,2,1,0:T(8,128)(2,1)}, u32[]{:S(2)}) copy-start(bf16[16,1,64,256]{3,2,1,0:T(8,128)(2,1)} %get-tuple-element.64) | copy-start | bytes 1572868
Sparse Core Ops, SparseCore 0:
  9.7 48.9 all-gather.1

commit v3 on v2

--- a/solution.py
+++ b/solution.py
@@ -5,6 +5,7 @@
 
 epsilon = 1e-05
 adapter_scale = 0.5
+UP_LAG = 0
 
 
 def ring_order(count):
@@ -13,6 +14,18 @@
 
 def tie(*values):
     return lax.optimization_barrier(values)
+
+
+def sum_parts(total):
+    count = lax.axis_size("tp")
+    if count & (count - 1):
+        return lax.psum(total, "tp")
+    bit = 1
+    while bit < count:
+        pairs = [(i, i ^ bit) for i in range(count)]
+        total = total + lax.ppermute(total.astype(jnp.bfloat16), "tp", pairs).astype(jnp.float32)
+        bit *= 2
+    return total
 
 
 def base_of(normed, *parts):
@@ -42,8 +55,6 @@
     my_place = jnp.asarray(place, jnp.int32)[me]
     order_table = jnp.asarray(order, jnp.int32)
 
-    up_all = lax.all_gather(adapter_up_weight, "ad", axis=0, tiled=True)
-
     pairs = jnp.arange(adapter_row_index.shape[0], dtype=jnp.int32)
     is_pair = language_pair_index[:, None] == pairs[None, :]
     slot_ids = jnp.sum(jnp.where(is_pair, adapter_row_index[None, :], 0), axis=1, keepdims=True)
@@ -64,10 +75,26 @@
         return total
 
     steps = owners // 2
+    up_f = up_b = adapter_up_weight
+    ups = [adapter_up_weight]
+    up_ids = [me * held + jnp.arange(held, dtype=jnp.int32)]
     half = held // 2
     up_block = down_block = adapter_down_weight
     low = term(adapter_down_weight, me * held)
     waiting = []
+
+    def carry_up(step):
+        nonlocal up_f, up_b
+        behind = order_table[lax.rem(my_place + owners - step, owners)] * held
+        ahead = order_table[lax.rem(my_place + step, owners)] * held
+        if step == steps:
+            up_f, up_b, ahead = up_f[:half], up_b[half:], ahead + half
+        up_f = lax.ppermute(up_f, "ad", forward)
+        up_b = lax.ppermute(up_b, "ad", backward)
+        ups.extend([up_f, up_b])
+        up_ids.append(behind + jnp.arange(up_f.shape[0], dtype=jnp.int32))
+        up_ids.append(ahead + jnp.arange(up_b.shape[0], dtype=jnp.int32))
+
     for step in range(1, steps + 1):
         from_behind = order_table[lax.rem(my_place + owners - step, owners)]
         from_ahead = order_table[lax.rem(my_place + step, owners)]
@@ -75,6 +102,8 @@
             up_block, down_block = up_block[:half], down_block[half:]
         up_next = lax.ppermute(up_block, "ad", forward)
         down_next = lax.ppermute(down_block, "ad", backward)
+        if step > UP_LAG:
+            carry_up(step - UP_LAG)
         if step == 2:
             key_value_weight, up_block, down_block = tie(key_value_weight, up_block, down_block)
             key_part, value_part = tie(key_value_weight[:, 0], key_value_weight[:, 1])
@@ -102,12 +131,20 @@
         else:
             low = low + term(up_next, from_behind * held)
             low = low + term(down_next, from_ahead * held + half)
+        if step < steps:
+            up_next, down_next, up_f, up_b = tie(up_next, down_next, up_f, up_b)
         up_block, down_block = up_next, down_next
 
-    low_rank = lax.psum(low, "tp").astype(jnp.bfloat16)
+    for step in range(max(steps - UP_LAG, 0) + 1, steps + 1):
+        if step == steps - UP_LAG + 1:
+            up_f, up_b, up_block, down_block = tie(up_f, up_b, up_block, down_block)
+        carry_up(step)
 
+    low_rank = sum_parts(low).astype(jnp.bfloat16)
+
+    up_all = jnp.concatenate(ups, axis=0)
     adapters = up_all.shape[0]
-    mask = slot_ids == jnp.arange(adapters, dtype=jnp.int32)[None, :]
+    mask = slot_ids == jnp.concatenate(up_ids)[None, :]
     halves = []
     for c in range(2):
         part = low_rank[:, c * rank : (c + 1) * rank]

time: 135 us -> 115 us (0.85)
  between operations: 22.8 us -> 9.35 us
  blocking collectives: 12.6 us -> 0 us
  starting transfers between devices: 9.21 us -> 19.1 us
  matrix products: 27.4 us -> 25.3 us
    psum x1 -> x0, blocking collectives: 12.6 us -> none  [on_device(): low_rank = lax.psum(low, 'tp').astype(jnp.bfloat16)]
    ppermute x0 -> x10, waiting for transfers between devices: none -> 10.8 us  [the longest x2 4.86 us: sum_parts(): lax.ppermute(total.astype(jnp.bfloat16), 'tp', pairs).astype(jnp.float32)]
    ppermute x0 -> x10, starting transfers between devices: none -> 9.83 us  [the longest x4 7.3 us: carry_up(): up_f = lax.ppermute(up_f, 'ad', forward)]
    ppermute x4, waiting for transfers between devices: 23.1 us -> 15.7 us  [on_device(): up_next = lax.ppermute(up_block, 'ad', forward)]
    ppermute x4, waiting for transfers between devices: 5.46 us -> 2.04 us  [on_device(): down_next = lax.ppermute(down_block, 'ad', backward)]
    slice x1, local copies, waits for them, and re-layouts: 2.09 us -> 0.1 us  [on_device(): up_all[:, c].reshape(adapters * rank, head_cols)]
    squeeze x1, local copies, waits for them, and re-layouts: 5.79 us -> 3.9 us  [on_device(): key_part, value_part = tie(key_value_weight[:, 0], key_value_weight[:, 1])]
    dot_general x2, matrix products: 7.39 us -> 5.75 us  [base_of(): jnp.dot(normed, part, preferred_element_type=jnp.float32)]
  transfers between devices with their start and end apart: 9 -> 18, of which waited for: 8 -> 8; matrix products, arithmetic and copies ran while one was open for 40% -> 44% of each run, Pallas kernels for 0% -> 0%
where the time goes in v3:
time: 115 us
  waiting for transfers between devices  28.6 us (25%)
  matrix products  25.3 us (22%)
  local copies, waits for them, and re-layouts  20.8 us (18%)
  starting transfers between devices  19.1 us (17%)
  other arithmetic  11.5 us (10%)
  between operations  9.35 us (8%)
    dot_general x16, matrix products, term(): low = jnp.dot(own_cols, block[j], preferred_element_type=jnp.float32)  18.6 us
    ppermute x4, waiting for transfers between devices, on_device(): up_next = lax.ppermute(up_block, 'ad', forward)  15.7 us
    ppermute x4, starting transfers between devices, on_device(): up_next = lax.ppermute(up_block, 'ad', forward)  8.3 us
    optimization_barrier x1, local copies, waits for them, and re-layouts, tie(): return lax.optimization_barrier(values)  7.84 us
    ppermute x4, starting transfers between devices, carry_up(): up_f = lax.ppermute(up_f, 'ad', forward)  7.3 us
    dot_general x2, matrix products, base_of(): jnp.dot(normed, part, preferred_element_type=jnp.float32)  5.75 us
    convert_element_type x1, other arithmetic, on_device(): (wide_hidden * inv_rms * gain.astype(jnp.float32)).astype(jnp.bfloat16)  5.5 us
    ppermute x2, waiting for transfers between devices, sum_parts(): lax.ppermute(total.astype(jnp.bfloat16), 'tp', pairs).astype(jnp.float32)  4.86 us
  transfers between devices with their start and end apart: 18, of which 8 were waited for; matrix products, arithmetic and copies ran while one was open for 44% of the time, Pallas kernels for 0%

profile of v3, /device:TPU:0, one launch (start us, length us, event | category | flops | bytes accessed | tf_op | source)
XLA Modules:
  0.0 114.6 jit_solution(2854737378774412714)
XLA Ops:
  0.0 3.0 %collective-permute-start = (bf16[2,2048,128]{2,1,0:T(8,128)(2,1)}, bf16[2,2048,128]{2,1,0:T(8,128)(2,1)}, u32[]{:S(2)}, u32[]{:S(2)}) collective-permute-start(bf16[2,2048,128]{2,1,0:T(8,128)(2,1)} %param.12), channel_id=1, source_target_pairs={{0,2},{2,4},{4,6},{6,7},{7,5},{5,3},{3,1},{1,0},{8,10},{10,12},{12... | collective-permute-start | bytes 3145736 | tf_op jit(solution)/shard_map/ppermute | solution.py:103
  3.0 2.0 %collective-permute-start.2 = (bf16[2,2,64,256]{3,2,1,0:T(8,128)(2,1)}, bf16[2,2,64,256]{3,2,1,0:T(8,128)(2,1)S(1)}, u32[]{:S(2)}, u32[]{:S(2)}) collective-permute-start(bf16[2,2,64,256]{3,2,1,0:T(8,128)(2,1)} %param.13), channel_id=1, source_target_pairs={{0,2},{2,4},{4,6},{6,7},{7,5},{5,3},{3,1},{1,0},{8,10},{10,12},{12... | collective-permute-start | bytes 393224 | tf_op jit(solution)/shard_map/ppermute | solution.py:92
  5.1 1.2 %dynamic_slice.37 = s32[1]{0:T(128)} dynamic-slice(s32[8]{0:T(128)} %constant.83.clone, s32[]{:T(128)S(6)} %select_n.120), dynamic_slice_sizes={1} | dynamic-slice | bytes 12 | tf_op jit(solution)/shard_map/dynamic_slice | solution.py:55
  10.9 1.6 %fusion.52 = (s32[1]{0:T(128)}, s32[1]{0:T(128)}, s32[1]{0:T(128)}, s32[1]{0:T(128)}, s32[1]{0:T(128)}, /*index=5*/s32[1]{0:T(128)}, s32[1]{0:T(128)}) fusion(s32[8]{0:T(128)} %constant.84.clone, s32[]{:T(128)S(6)} %select_n.121, s32[]{:T(128)S(6)} %select_n.133, s32[]{:T(128)S(6)} %select_n.130, s32[]{:T(128)S(6)} %select_n.127, s32[]{:T(128)S(6)} %select_n.124, ...), kind=kLoop, calls=%fused_computation.117 | loop fusion | bytes 84 | tf_op jit(solution)/shard_map/dynamic_slice | solution.py:99
  16.8 0.7 convert_element_type.43
  17.6 4.6 %fusion = f32[448]{0:T(512)S(1)} fusion(bf16[448,8192]{1,0:T(8,128)(2,1)} %param.9), kind=kLoop, calls=%fused_computation.2 | loop fusion | flops 11009600 | bytes 7341824 | tf_op jit(solution)/shard_map/reduce_sum | solution.py:63
  22.2 5.5 %fusion.2 = bf16[448,8192]{1,0:T(8,128)(2,1)S(1)} fusion(bf16[448,8192]{1,0:T(8,128)(2,1)} %param.9, f32[8192]{0:T(1024)S(1)} %convert_element_type.43, f32[448]{0:T(512)S(1)} %add_rsqrt_fusion), kind=kLoop, calls=%fused_computation.4 | loop fusion | flops 14680064 | bytes 14714624 | tf_op jit(solution)/shard_map/convert_element_type | solution.py:64
  27.7 3.0 %copy-done = bf16[448,8192]{1,0:T(8,128)(2,1)} copy-done((bf16[448,8192]{1,0:T(8,128)(2,1)}, bf16[448,8192]{1,0:T(8,128)(2,1)S(1)}, u32[]{:S(2)}) %copy-start) | copy-done | bytes 7340056
  30.7 0.2 constant_dynamic-slice_fusion
  30.9 0.5 copy-done.5
  31.4 0.1 select_reduce_fusion
  31.5 0.1 compare_reduce_fusion
  31.6 0.1 concatenate.6
  31.7 0.3 copy-done.3
  32.0 0.6 convolution_select_fusion.15
  32.6 0.6 fusion.14
  33.3 0.2 copy-done.4
  33.6 2.1 %collective-permute-start.4 = (bf16[2,2048,128]{2,1,0:T(8,128)(2,1)}, bf16[2,2048,128]{2,1,0:T(8,128)(2,1)}, u32[]{:S(2)}, u32[]{:S(2)}) collective-permute-start(bf16[2,2048,128]{2,1,0:T(8,128)(2,1)} %collective-permute-done), channel_id=1, source_target_pairs={{0,2},{2,4},{4,6},{6,7},{7,5},{5,3},{3,1},{1,0},{8,10},{10,12},{12... | collective-permute-start | bytes 3145736 | tf_op jit(solution)/shard_map/ppermute | solution.py:103
  35.7 7.8 %copy.16 = bf16[8192,2,256]{2,0,1:T(8,128)(2,1)} copy(bf16[8192,2,256]{2,1,0:T(2,128)(2,1)} %param.11) | data formatting | bytes 16777216 | tf_op jit(solution)/shard_map/optimization_barrier | solution.py:16
  43.5 3.9 %slice_bitcast_fusion = (bf16[8192,256]{1,0:T(8,128)(2,1)S(1)}, bf16[8192,256]{1,0:T(8,128)(2,1)S(1)}) fusion(bf16[8192,2,256]{2,0,1:T(8,128)(2,1)} %copy.16), kind=kLoop, calls=%fused_computation.5 | loop fusion | bytes 16777216 | tf_op jit(solution)/shard_map/squeeze | solution.py:109
  47.4 2.1 %collective-permute-start.6 = (bf16[2,2,64,256]{3,2,1,0:T(8,128)(2,1)S(1)}, bf16[2,2,64,256]{3,2,1,0:T(8,128)(2,1)S(1)}, u32[]{:S(2)}, u32[]{:S(2)}) collective-permute-start(bf16[2,2,64,256]{3,2,1,0:T(8,128)(2,1)S(1)} %collective-permute-done.2), channel_id=1, source_target_pairs={{0,2},{2,4},{4,6},{6,7},{7,5},{5,3},{3,1},{1,0},{8,10},{10,12},{12... | collective-permute-start | bytes 393224 | tf_op jit(solution)/shard_map/ppermute | solution.py:92
  49.5 1.7 %convolution_select_fusion.13 = f32[448,128]{1,0:T(8,128)S(1)} fusion(bf16[448,2048]{1,0:T(8,128)(2,1)S(1)} %constant_dynamic-slice_fusion, bf16[2,2048,128]{2,1,0:T(8,128)(2,1)} %collective-permute-done, pred[448]{0:T(512)(128)(4,1)S(1)} %get-tuple-element.82), kind=kOutput, calls=%fused_computation.33 | convolution fusion | flops 234938368 | bytes 2589120 | tf_op jit(solution)/shard_map/dot_general | solution.py:73
  51.2 1.7 %convolution_select_fusion.11 = f32[448,128]{1,0:T(8,128)S(1)} fusion(bf16[448,2048]{1,0:T(8,128)(2,1)S(1)} %constant_dynamic-slice_fusion, bf16[2,2048,128]{2,1,0:T(8,128)(2,1)} %collective-permute-done.1, pred[448]{0:T(512)(128)(4,1)S(1)} %get-tuple-element.80), kind=kOutput, calls=%fused_computation.30 | convolution fusion | flops 234938368 | bytes 2589120 | tf_op jit(solution)/shard_map/dot_general | solution.py:73
  52.9 1.7 %fusion.13 = f32[448,128]{1,0:T(8,128)S(1)} fusion(f32[448,128]{1,0:T(8,128)S(1)} %convolution_select_fusion.13, bf16[448,2048]{1,0:T(8,128)(2,1)S(1)} %constant_dynamic-slice_fusion, bf16[2,2048,128]{2,1,0:T(8,128)(2,1)} %collective-permute-done, pred[448]{0:T(512)(128)(4,1)S(1)} %get-tuple-element.81), kind=kOutput, calls=%fused_computation.32 | convolution fusion | flops 234995712 | bytes 2818496 | tf_op jit(solution)/shard_map/dot_general | solution.py:73
  54.6 1.7 %fusion.12 = f32[448,128]{1,0:T(8,128)S(1)} fusion(f32[448,128]{1,0:T(8,128)S(1)} %convolution_select_fusion.11, bf16[448,2048]{1,0:T(8,128)(2,1)S(1)} %constant_dynamic-slice_fusion, bf16[2,2048,128]{2,1,0:T(8,128)(2,1)} %collective-permute-done.1, pred[448]{0:T(512)(128)(4,1)S(1)} %get-tuple-element.79), kind=kOutput, calls=%fused_computation.29 | convolution fusion | flops 234995712 | bytes 2818496 | tf_op jit(solution)/shard_map/dot_general | solution.py:73
  56.3 4.4 %collective-permute-done.6 = bf16[2,2,64,256]{3,2,1,0:T(8,128)(2,1)S(1)} collective-permute-done((bf16[2,2,64,256]{3,2,1,0:T(8,128)(2,1)S(1)}, bf16[2,2,64,256]{3,2,1,0:T(8,128)(2,1)S(1)}, u32[]{:S(2)}, u32[]{:S(2)}) %collective-permute-start.6) | collective-permute-done | bytes 131104 | tf_op jit(solution)/shard_map/ppermute | solution.py:92
  60.7 1.4 %collective-permute-done.7 = bf16[2,2,64,256]{3,2,1,0:T(8,128)(2,1)S(1)} collective-permute-done((bf16[2,2,64,256]{3,2,1,0:T(8,128)(2,1)S(1)}, bf16[2,2,64,256]{3,2,1,0:T(8,128)(2,1)S(1)}, u32[]{:S(2)}, u32[]{:S(2)}) %collective-permute-start.7) | collective-permute-done | bytes 131104 | tf_op jit(solution)/shard_map/ppermute | solution.py:93
  62.2 1.6 %collective-permute-start.10 = (bf16[2,2,64,256]{3,2,1,0:T(8,128)(2,1)S(1)}, bf16[2,2,64,256]{3,2,1,0:T(8,128)(2,1)S(1)}, u32[]{:S(2)}, u32[]{:S(2)}) collective-permute-start(bf16[2,2,64,256]{3,2,1,0:T(8,128)(2,1)S(1)} %collective-permute-done.6), channel_id=1, source_target_pairs={{0,2},{2,4},{4,6},{6,7},{7,5},{5,3},{3,1},{1,0},{8,10},{10,12},{12... | collective-permute-start | bytes 393224 | tf_op jit(solution)/shard_map/ppermute | solution.py:92
  63.9 0.4 collective-permute-start.11
  64.3 1.6 %collective-permute-start.8 = (bf16[2,2048,128]{2,1,0:T(8,128)(2,1)}, bf16[2,2048,128]{2,1,0:T(8,128)(2,1)S(1)}, u32[]{:S(2)}, u32[]{:S(2)}) collective-permute-start(bf16[2,2048,128]{2,1,0:T(8,128)(2,1)} %collective-permute-done.4), channel_id=1, source_target_pairs={{0,2},{2,4},{4,6},{6,7},{7,5},{5,3},{3,1},{1,0},{8,10},{10,12},{12... | collective-permute-start | bytes 3145736 | tf_op jit(solution)/shard_map/ppermute | solution.py:103
  65.9 0.4 collective-permute-start.9
  66.3 2.9 %fusion.55 = f32[448,256]{1,0:T(8,128)} fusion(bf16[448,8192]{1,0:T(8,128)(2,1)S(1)} %bitcast.106, bf16[8192,256]{1,0:T(8,128)(2,1)S(1)} %get-tuple-element.57), kind=kOutput, calls=%fused_computation.120 | convolution fusion | flops 1879048192 | bytes 11993088 | tf_op jit(solution)/shard_map/dot_general | solution.py:32
  69.2 2.9 %fusion.54 = f32[448,256]{1,0:T(8,128)} fusion(bf16[448,8192]{1,0:T(8,128)(2,1)S(1)} %bitcast.106, bf16[8192,256]{1,0:T(8,128)(2,1)S(1)} %get-tuple-element.56), kind=kOutput, calls=%fused_computation.119 | convolution fusion | flops 1879048192 | bytes 11993088 | tf_op jit(solution)/shard_map/dot_general | solution.py:32
  72.1 1.7 %convolution_select_fusion.9 = f32[448,128]{1,0:T(8,128)S(1)} fusion(bf16[448,2048]{1,0:T(8,128)(2,1)S(1)} %constant_dynamic-slice_fusion, bf16[2,2048,128]{2,1,0:T(8,128)(2,1)} %collective-permute-done.4, pred[448]{0:T(512)(128)(4,1)S(1)} %get-tuple-element.78), kind=kOutput, calls=%fused_computation.27 | convolution fusion | flops 234938368 | bytes 2589120 | tf_op jit(solution)/shard_map/dot_general | solution.py:73
  73.8 1.7 %convolution_select_fusion.7 = f32[448,128]{1,0:T(8,128)S(1)} fusion(bf16[448,2048]{1,0:T(8,128)(2,1)S(1)} %constant_dynamic-slice_fusion, bf16[2,2048,128]{2,1,0:T(8,128)(2,1)} %collective-permute-done.5, pred[448]{0:T(512)(128)(4,1)S(1)} %get-tuple-element.76), kind=kOutput, calls=%fused_computation.24 | convolution fusion | flops 234938368 | bytes 2589120 | tf_op jit(solution)/shard_map/dot_general | solution.py:73
  75.5 1.7 %fusion.11 = f32[448,128]{1,0:T(8,128)S(1)} fusion(f32[448,128]{1,0:T(8,128)S(1)} %convolution_select_fusion.9, bf16[448,2048]{1,0:T(8,128)(2,1)S(1)} %constant_dynamic-slice_fusion, bf16[2,2048,128]{2,1,0:T(8,128)(2,1)} %collective-permute-done.4, pred[448]{0:T(512)(128)(4,1)S(1)} %get-tuple-element.77), kind=kOutput, calls=%fused_computation.26 | convolution fusion | flops 234995712 | bytes 2818496 | tf_op jit(solution)/shard_map/dot_general | solution.py:73
  77.2 1.7 %fusion.10 = f32[448,128]{1,0:T(8,128)S(1)} fusion(f32[448,128]{1,0:T(8,128)S(1)} %convolution_select_fusion.7, bf16[448,2048]{1,0:T(8,128)(2,1)S(1)} %constant_dynamic-slice_fusion, bf16[2,2048,128]{2,1,0:T(8,128)(2,1)} %collective-permute-done.5, f32[448,128]{1,0:T(8,128)S(1)} %fusion.11, f32[448,128]{1,0:T(8,128)S(1)} %fusion.12, ...), kind=kOutput, calls=%fused_computation.23 | convolution fusion | flops 235225088 | bytes 3736000 | tf_op jit(solution)/shard_map/dot_general | solution.py:73
  78.9 9.1 %collective-permute-done.8 = bf16[2,2048,128]{2,1,0:T(8,128)(2,1)S(1)} collective-permute-done((bf16[2,2048,128]{2,1,0:T(8,128)(2,1)}, bf16[2,2048,128]{2,1,0:T(8,128)(2,1)S(1)}, u32[]{:S(2)}, u32[]{:S(2)}) %collective-permute-start.8) | collective-permute-done | bytes 1048608 | tf_op jit(solution)/shard_map/ppermute | solution.py:103
  88.0 1.3 %collective-permute-done.9 = bf16[2,2048,128]{2,1,0:T(8,128)(2,1)S(1)} collective-permute-done((bf16[2,2048,128]{2,1,0:T(8,128)(2,1)}, bf16[2,2048,128]{2,1,0:T(8,128)(2,1)S(1)}, u32[]{:S(2)}, u32[]{:S(2)}) %collective-permute-start.9) | collective-permute-done | bytes 1048608 | tf_op jit(solution)/shard_map/ppermute | solution.py:104
  89.3 1.6 %collective-permute-start.16 = (bf16[1,2,64,256]{3,2,1,0:T(8,128)(2,1)S(1)}, bf16[1,2,64,256]{3,2,1,0:T(8,128)(2,1)S(1)}, u32[]{:S(2)}, u32[]{:S(2)}) collective-permute-start(bf16[1,2,64,256]{3,2,1,0:T(8,128)(2,1)S(1)} %slice.91), channel_id=1, source_target_pairs={{0,2},{2,4},{4,6},{6,7},{7,5},{5,3},{3,1},{1,0},{8,10},{10,12},{12... | collective-permute-start | bytes 196616 | tf_op jit(solution)/shard_map/ppermute | solution.py:92
  90.9 0.4 collective-permute-start.17
  91.4 0.6 convolution_select_fusion.5
  92.1 1.6 %collective-permute-start.12 = (bf16[1,2048,128]{2,1,0:T(8,128)(2,1)S(1)}, bf16[1,2048,128]{2,1,0:T(8,128)(2,1)S(1)}, u32[]{:S(2)}, u32[]{:S(2)}) collective-permute-start(bf16[1,2048,128]{2,1,0:T(8,128)(2,1)S(1)} %slice.88), channel_id=1, source_target_pairs={{0,2},{2,4},{4,6},{6,7},{7,5},{5,3},{3,1},{1,0},{8,10},{10,12},{12... | collective-permute-start | bytes 1572872 | tf_op jit(solution)/shard_map/ppermute | solution.py:103
  93.7 0.5 collective-permute-start.13
  94.2 0.6 fusion.8
  94.9 0.6 convolution_select_fusion.3
  95.5 0.6 fusion.7
  96.2 6.6 %collective-permute-done.12 = bf16[1,2048,128]{2,1,0:T(8,128)(2,1)S(1)} collective-permute-done((bf16[1,2048,128]{2,1,0:T(8,128)(2,1)S(1)}, bf16[1,2048,128]{2,1,0:T(8,128)(2,1)S(1)}, u32[]{:S(2)}, u32[]{:S(2)}) %collective-permute-start.12) | collective-permute-done | bytes 524320 | tf_op jit(solution)/shard_map/ppermute | solution.py:103
  102.8 0.6 convolution_select_fusion.1
  103.4 0.7 collective-permute-done.13
  104.2 0.6 fusion.53
  104.9 1.3 %collective-permute-done.14 = bf16[448,128]{1,0:T(8,128)(2,1)S(1)} collective-permute-done((bf16[448,128]{1,0:T(8,128)(2,1)S(1)}, bf16[448,128]{1,0:T(8,128)(2,1)S(1)}, u32[]{:S(2)}, u32[]{:S(2)}) %collective-permute-start.14) | collective-permute-done | bytes 114720 | tf_op jit(solution)/shard_map/ppermute | solution.py:26
  106.2 1.6 %collective-permute-start.15 = (bf16[448,128]{1,0:T(8,128)(2,1)S(1)}, bf16[448,128]{1,0:T(8,128)(2,1)S(1)}, u32[]{:S(2)}, u32[]{:S(2)}) collective-permute-start(bf16[448,128]{1,0:T(8,128)(2,1)S(1)} %fusion.47), channel_id=1, source_target_pairs={{0,16},{8,24},{16,0},{24,8},{1,17},{9,25},{17,1},{25,9},{2,18},{10... | collective-permute-start | bytes 344072 | tf_op jit(solution)/shard_map/ppermute | solution.py:26
  107.8 0.1 fusion.50
  107.9 3.6 %collective-permute-done.15 = bf16[448,128]{1,0:T(8,128)(2,1)S(1)} collective-permute-done((bf16[448,128]{1,0:T(8,128)(2,1)S(1)}, bf16[448,128]{1,0:T(8,128)(2,1)S(1)}, u32[]{:S(2)}, u32[]{:S(2)}) %collective-permute-start.15) | collective-permute-done | bytes 114720 | tf_op jit(solution)/shard_map/ppermute | solution.py:26
  111.6 0.1 fusion.51
  111.7 0.1 copy.18
  111.8 0.1 copy.19
  111.9 0.1 broadcast_select_fusion.1
  112.0 0.5 fusion.4
  112.5 0.5 fusion.6
  113.0 0.1 copy-done.2
  113.2 0.1 fusion.45
  113.4 1.2 %copy.20 = bf16[448,2,256]{2,1,0:T(2,128)(2,1)} copy(bf16[448,2,256]{2,0,1:T(8,128)(2,1)S(1)} %pad_maximum_fusion) | data formatting | bytes 917504 | tf_op jit(solution)/shard_map/stack | solution.py:163
  (54 shorter events, 0.6 us)
Async XLA Ops:
  0.0 33.6 %collective-permute-start = (bf16[2,2048,128]{2,1,0:T(8,128)(2,1)}, bf16[2,2048,128]{2,1,0:T(8,128)(2,1)}, u32[]{:S(2)}, u32[]{:S(2)}) collective-permute-start(bf16[2,2048,128]{2,1,0:T(8,128)(2,1)} %param.12), channel_id=1, source_target_pairs={{0,2},{2,4},{4,6},{6,7},{7,5},{5,3},{3,1},{1,0},{8,10},{10,12},{12... | collective-permute-start | bytes 3145736 | tf_op jit(solution)/shard_map/ppermute | solution.py:103
  3.0 30.6 %collective-permute-start.1 = (bf16[2,2048,128]{2,1,0:T(8,128)(2,1)}, bf16[2,2048,128]{2,1,0:T(8,128)(2,1)}, u32[]{:S(2)}, u32[]{:S(2)}) collective-permute-start(bf16[2,2048,128]{2,1,0:T(8,128)(2,1)} %param.12), channel_id=1, source_target_pairs={{2,0},{4,2},{6,4},{7,6},{5,7},{3,5},{1,3},{0,1},{10,8},{12,10},{14... | collective-permute-start | bytes 3145736 | tf_op jit(solution)/shard_map/ppermute | solution.py:104
  3.0 30.5 %collective-permute-start.2 = (bf16[2,2,64,256]{3,2,1,0:T(8,128)(2,1)}, bf16[2,2,64,256]{3,2,1,0:T(8,128)(2,1)S(1)}, u32[]{:S(2)}, u32[]{:S(2)}) collective-permute-start(bf16[2,2,64,256]{3,2,1,0:T(8,128)(2,1)} %param.13), channel_id=1, source_target_pairs={{0,2},{2,4},{4,6},{6,7},{7,5},{5,3},{3,1},{1,0},{8,10},{10,12},{12... | collective-permute-start | bytes 393224 | tf_op jit(solution)/shard_map/ppermute | solution.py:92
  5.1 28.5 %collective-permute-start.3 = (bf16[2,2,64,256]{3,2,1,0:T(8,128)(2,1)}, bf16[2,2,64,256]{3,2,1,0:T(8,128)(2,1)S(1)}, u32[]{:S(2)}, u32[]{:S(2)}) collective-permute-start(bf16[2,2,64,256]{3,2,1,0:T(8,128)(2,1)} %param.13), channel_id=1, source_target_pairs={{2,0},{4,2},{6,4},{7,6},{5,7},{3,5},{1,3},{0,1},{10,8},{12,10},{14... | collective-permute-start | bytes 393224 | tf_op jit(solution)/shard_map/ppermute | solution.py:93
  27.7 3.0 %copy-start = (bf16[448,8192]{1,0:T(8,128)(2,1)}, bf16[448,8192]{1,0:T(8,128)(2,1)S(1)}, u32[]{:S(2)}) copy-start(bf16[448,8192]{1,0:T(8,128)(2,1)S(1)} %fusion.2) | copy-start | bytes 22020100
  30.7 0.7 copy-start.5
  30.7 0.7 copy-start.6
  30.7 1.3 %copy-start.3 = (bf16[2,2048,128]{2,1,0:T(8,128)(2,1)S(1)}, bf16[2,2048,128]{2,1,0:T(8,128)(2,1)}, u32[]{:S(2)}) copy-start(bf16[2,2048,128]{2,1,0:T(8,128)(2,1)} %param.12) | copy-start | bytes 3145732
  32.6 0.9 copy-start.4
  33.6 28.6 %collective-permute-start.4 = (bf16[2,2048,128]{2,1,0:T(8,128)(2,1)}, bf16[2,2048,128]{2,1,0:T(8,128)(2,1)}, u32[]{:S(2)}, u32[]{:S(2)}) collective-permute-start(bf16[2,2048,128]{2,1,0:T(8,128)(2,1)} %collective-permute-done), channel_id=1, source_target_pairs={{0,2},{2,4},{4,6},{6,7},{7,5},{5,3},{3,1},{1,0},{8,10},{10,12},{12... | collective-permute-start | bytes 3145736 | tf_op jit(solution)/shard_map/ppermute | solution.py:103
  35.7 26.5 %collective-permute-start.5 = (bf16[2,2048,128]{2,1,0:T(8,128)(2,1)}, bf16[2,2048,128]{2,1,0:T(8,128)(2,1)}, u32[]{:S(2)}, u32[]{:S(2)}) collective-permute-start(bf16[2,2048,128]{2,1,0:T(8,128)(2,1)} %collective-permute-done.1), channel_id=1, source_target_pairs={{2,0},{4,2},{6,4},{7,6},{5,7},{3,5},{1,3},{0,1},{10,8},{12,10},{14... | collective-permute-start | bytes 3145736 | tf_op jit(solution)/shard_map/ppermute | solution.py:104
  35.7 30.7 %slice-start = ((s8[7340032]{0:T(1024)(128)(4,1)}), s8[3145728]{0:T(1024)(128)(4,1)S(1)}, s32[]{:S(2)}) async-start(s8[7340032]{0:T(1024)(128)(4,1)} %bitcast.105), calls=%async_computation | async-start | bytes 6291456
  43.5 22.8 %slice-start.1 = ((s8[7340032]{0:T(1024)(128)(4,1)}), s8[4194304]{0:T(1024)(128)(4,1)S(1)}, s32[]{:S(2)}) async-start(s8[7340032]{0:T(1024)(128)(4,1)} %bitcast.105), calls=%async_computation.1 | async-start | bytes 8388608
  47.4 13.3 %collective-permute-start.6 = (bf16[2,2,64,256]{3,2,1,0:T(8,128)(2,1)S(1)}, bf16[2,2,64,256]{3,2,1,0:T(8,128)(2,1)S(1)}, u32[]{:S(2)}, u32[]{:S(2)}) collective-permute-start(bf16[2,2,64,256]{3,2,1,0:T(8,128)(2,1)S(1)} %collective-permute-done.2), channel_id=1, source_target_pairs={{0,2},{2,4},{4,6},{6,7},{7,5},{5,3},{3,1},{1,0},{8,10},{10,12},{12... | collective-permute-start | bytes 393224 | tf_op jit(solution)/shard_map/ppermute | solution.py:92
  49.5 12.7 %collective-permute-start.7 = (bf16[2,2,64,256]{3,2,1,0:T(8,128)(2,1)S(1)}, bf16[2,2,64,256]{3,2,1,0:T(8,128)(2,1)S(1)}, u32[]{:S(2)}, u32[]{:S(2)}) collective-permute-start(bf16[2,2,64,256]{3,2,1,0:T(8,128)(2,1)S(1)} %collective-permute-done.3), channel_id=1, source_target_pairs={{2,0},{4,2},{6,4},{7,6},{5,7},{3,5},{1,3},{0,1},{10,8},{12,10},{14... | collective-permute-start | bytes 393224 | tf_op jit(solution)/shard_map/ppermute | solution.py:93
  62.2 16.6 %collective-permute-start.10 = (bf16[2,2,64,256]{3,2,1,0:T(8,128)(2,1)S(1)}, bf16[2,2,64,256]{3,2,1,0:T(8,128)(2,1)S(1)}, u32[]{:S(2)}, u32[]{:S(2)}) collective-permute-start(bf16[2,2,64,256]{3,2,1,0:T(8,128)(2,1)S(1)} %collective-permute-done.6), channel_id=1, source_target_pairs={{0,2},{2,4},{4,6},{6,7},{7,5},{5,3},{3,1},{1,0},{8,10},{10,12},{12... | collective-permute-start | bytes 393224 | tf_op jit(solution)/shard_map/ppermute | solution.py:92
  63.9 15.0 %collective-permute-start.11 = (bf16[2,2,64,256]{3,2,1,0:T(8,128)(2,1)S(1)}, bf16[2,2,64,256]{3,2,1,0:T(8,128)(2,1)S(1)}, u32[]{:S(2)}, u32[]{:S(2)}) collective-permute-start(bf16[2,2,64,256]{3,2,1,0:T(8,128)(2,1)S(1)} %collective-permute-done.7), channel_id=1, source_target_pairs={{2,0},{4,2},{6,4},{7,6},{5,7},{3,5},{1,3},{0,1},{10,8},{12,10},{14... | collective-permute-start | bytes 393224 | tf_op jit(solution)/shard_map/ppermute | solution.py:93
  64.3 23.7 %collective-permute-start.8 = (bf16[2,2048,128]{2,1,0:T(8,128)(2,1)}, bf16[2,2048,128]{2,1,0:T(8,128)(2,1)S(1)}, u32[]{:S(2)}, u32[]{:S(2)}) collective-permute-start(bf16[2,2048,128]{2,1,0:T(8,128)(2,1)} %collective-permute-done.4), channel_id=1, source_target_pairs={{0,2},{2,4},{4,6},{6,7},{7,5},{5,3},{3,1},{1,0},{8,10},{10,12},{12... | collective-permute-start | bytes 3145736 | tf_op jit(solution)/shard_map/ppermute | solution.py:103
  65.9 23.5 %collective-permute-start.9 = (bf16[2,2048,128]{2,1,0:T(8,128)(2,1)}, bf16[2,2048,128]{2,1,0:T(8,128)(2,1)S(1)}, u32[]{:S(2)}, u32[]{:S(2)}) collective-permute-start(bf16[2,2048,128]{2,1,0:T(8,128)(2,1)} %collective-permute-done.5), channel_id=1, source_target_pairs={{2,0},{4,2},{6,4},{7,6},{5,7},{3,5},{1,3},{0,1},{10,8},{12,10},{14... | collective-permute-start | bytes 3145736 | tf_op jit(solution)/shard_map/ppermute | solution.py:104
  89.3 15.6 %collective-permute-start.16 = (bf16[1,2,64,256]{3,2,1,0:T(8,128)(2,1)S(1)}, bf16[1,2,64,256]{3,2,1,0:T(8,128)(2,1)S(1)}, u32[]{:S(2)}, u32[]{:S(2)}) collective-permute-start(bf16[1,2,64,256]{3,2,1,0:T(8,128)(2,1)S(1)} %slice.91), channel_id=1, source_target_pairs={{0,2},{2,4},{4,6},{6,7},{7,5},{5,3},{3,1},{1,0},{8,10},{10,12},{12... | collective-permute-start | bytes 196616 | tf_op jit(solution)/shard_map/ppermute | solution.py:92
  90.9 14.0 %collective-permute-start.17 = (bf16[1,2,64,256]{3,2,1,0:T(8,128)(2,1)S(1)}, bf16[1,2,64,256]{3,2,1,0:T(8,128)(2,1)S(1)}, u32[]{:S(2)}, u32[]{:S(2)}) collective-permute-start(bf16[1,2,64,256]{3,2,1,0:T(8,128)(2,1)S(1)} %slice.92), channel_id=1, source_target_pairs={{2,0},{4,2},{6,4},{7,6},{5,7},{3,5},{1,3},{0,1},{10,8},{12,10},{14... | collective-permute-start | bytes 196616 | tf_op jit(solution)/shard_map/ppermute | solution.py:93
  92.1 10.7 %collective-permute-start.12 = (bf16[1,2048,128]{2,1,0:T(8,128)(2,1)S(1)}, bf16[1,2048,128]{2,1,0:T(8,128)(2,1)S(1)}, u32[]{:S(2)}, u32[]{:S(2)}) collective-permute-start(bf16[1,2048,128]{2,1,0:T(8,128)(2,1)S(1)} %slice.88), channel_id=1, source_target_pairs={{0,2},{2,4},{4,6},{6,7},{7,5},{5,3},{3,1},{1,0},{8,10},{10,12},{12... | collective-permute-start | bytes 1572872 | tf_op jit(solution)/shard_map/ppermute | solution.py:103
  93.7 10.4 %collective-permute-start.13 = (bf16[1,2048,128]{2,1,0:T(8,128)(2,1)S(1)}, bf16[1,2048,128]{2,1,0:T(8,128)(2,1)S(1)}, u32[]{:S(2)}, u32[]{:S(2)}) collective-permute-start(bf16[1,2048,128]{2,1,0:T(8,128)(2,1)S(1)} %slice.89), channel_id=1, source_target_pairs={{2,0},{4,2},{6,4},{7,6},{5,7},{3,5},{1,3},{0,1},{10,8},{12,10},{14... | collective-permute-start | bytes 1572872 | tf_op jit(solution)/shard_map/ppermute | solution.py:104
  104.8 1.4 %collective-permute-start.14 = (bf16[448,128]{1,0:T(8,128)(2,1)S(1)}, bf16[448,128]{1,0:T(8,128)(2,1)S(1)}, u32[]{:S(2)}, u32[]{:S(2)}) collective-permute-start(bf16[448,128]{1,0:T(8,128)(2,1)S(1)} %get-tuple-element.100), channel_id=1, source_target_pairs={{0,8},{8,0},{16,24},{24,16},{1,9},{9,1},{17,25},{25,17},{2,10},{10... | collective-permute-start | bytes 344072 | tf_op jit(solution)/shard_map/ppermute | solution.py:26
  106.2 5.3 %collective-permute-start.15 = (bf16[448,128]{1,0:T(8,128)(2,1)S(1)}, bf16[448,128]{1,0:T(8,128)(2,1)S(1)}, u32[]{:S(2)}, u32[]{:S(2)}) collective-permute-start(bf16[448,128]{1,0:T(8,128)(2,1)S(1)} %fusion.47), channel_id=1, source_target_pairs={{0,16},{8,24},{16,0},{24,8},{1,17},{9,25},{17,1},{25,9},{2,18},{10... | collective-permute-start | bytes 344072 | tf_op jit(solution)/shard_map/ppermute | solution.py:26
  112.0 1.0 copy-start.1
  112.0 1.1 %copy-start.2 = (f32[448,256]{1,0:T(8,128)S(1)}, f32[448,256]{1,0:T(8,128)}, u32[]{:S(2)}) copy-start(f32[448,256]{1,0:T(8,128)} %fusion.54) | copy-start | bytes 1376260

commit v4 on v3

--- a/solution.py
+++ b/solution.py
@@ -5,7 +5,6 @@
 
 epsilon = 1e-05
 adapter_scale = 0.5
-UP_LAG = 0
 
 
 def ring_order(count):
@@ -51,9 +50,11 @@
     order = ring_order(owners)
     forward = [(order[i], order[(i + 1) % owners]) for i in range(owners)]
     backward = [(b, a) for a, b in forward]
-    place = [order.index(i) for i in range(owners)]
-    my_place = jnp.asarray(place, jnp.int32)[me]
-    order_table = jnp.asarray(order, jnp.int32)
+    my_place = jnp.where(me % 2 == 0, me // 2, owners - 1 - me // 2)
+    evens = (owners + 1) // 2
+
+    def owner_at(place_of):
+        return jnp.where(place_of < evens, 2 * place_of, 2 * (owners - place_of) - 1)
 
     pairs = jnp.arange(adapter_row_index.shape[0], dtype=jnp.int32)
     is_pair = language_pair_index[:, None] == pairs[None, :]
@@ -65,7 +66,7 @@
     own_cols = lax.dynamic_slice_in_dim(
         normed, lax.axis_index("tp") * column_portion, column_portion, 1
     )
-    own_cols, normed, slot_ids = tie(own_cols, normed, slot_ids)
+    own_cols, normed = tie(own_cols, normed)
 
     def term(block, first_id):
         total = jnp.float32(0.0)
@@ -80,13 +81,13 @@
     up_ids = [me * held + jnp.arange(held, dtype=jnp.int32)]
     half = held // 2
     up_block = down_block = adapter_down_weight
-    low = term(adapter_down_weight, me * held)
-    waiting = []
+    low = jnp.zeros((tok_count, low_width), jnp.float32)
+    waiting = [(adapter_down_weight, me)]
 
     def carry_up(step):
         nonlocal up_f, up_b
-        behind = order_table[lax.rem(my_place + owners - step, owners)] * held
-        ahead = order_table[lax.rem(my_place + step, owners)] * held
+        behind = owner_at(lax.rem(my_place + owners - step, owners)) * held
+        ahead = owner_at(lax.rem(my_place + step, owners)) * held
         if step == steps:
             up_f, up_b, ahead = up_f[:half], up_b[half:], ahead + half
         up_f = lax.ppermute(up_f, "ad", forward)
@@ -96,14 +97,13 @@
         up_ids.append(ahead + jnp.arange(up_b.shape[0], dtype=jnp.int32))
 
     for step in range(1, steps + 1):
-        from_behind = order_table[lax.rem(my_place + owners - step, owners)]
-        from_ahead = order_table[lax.rem(my_place + step, owners)]
+        from_behind = owner_at(lax.rem(my_place + owners - step, owners))
+        from_ahead = owner_at(lax.rem(my_place + step, owners))
         if step == steps:
             up_block, down_block = up_block[:half], down_block[half:]
         up_next = lax.ppermute(up_block, "ad", forward)
         down_next = lax.ppermute(down_block, "ad", backward)
-        if step > UP_LAG:
-            carry_up(step - UP_LAG)
+        carry_up(step)
         if step == 2:
             key_value_weight, up_block, down_block = tie(key_value_weight, up_block, down_block)
             key_part, value_part = tie(key_value_weight[:, 0], key_value_weight[:, 1])
@@ -118,7 +118,7 @@
             waiting = []
         if step < steps:
             if step == 1:
-                up_next, down_next, low = tie(up_next, down_next, low)
+                up_next, down_next, own_cols = tie(up_next, down_next, own_cols)
             elif step == 2:
                 up_next, down_next, key_part, value_part = tie(
                     up_next, down_next, key_part, value_part
@@ -134,11 +134,6 @@
         if step < steps:
             up_next, down_next, up_f, up_b = tie(up_next, down_next, up_f, up_b)
         up_block, down_block = up_next, down_next
-
-    for step in range(max(steps - UP_LAG, 0) + 1, steps + 1):
-        if step == steps - UP_LAG + 1:
-            up_f, up_b, up_block, down_block = tie(up_f, up_b, up_block, down_block)
-        carry_up(step)
 
     low_rank = sum_parts(low).astype(jnp.bfloat16)
 

time: 115 us -> 111 us (0.965)
  waiting for transfers between devices: 28.6 us -> 43.8 us
  between operations: 9.35 us -> 0.51 us
  matrix products: 25.3 us -> 17.5 us
  local copies, waits for them, and re-layouts: 20.8 us -> 15.1 us
  other arithmetic: 11.5 us -> 14.6 us
    ppermute x4, waiting for transfers between devices: 4.46 us -> 14.9 us  [carry_up(): up_f = lax.ppermute(up_f, 'ad', forward)]
    dot_general x16, matrix products: 18.6 us -> 12.4 us  [term(): low = jnp.dot(own_cols, block[j], preferred_element_type=jnp.float32)]
    unnamed x26 -> x20, local copies, waits for them, and re-layouts: 4.21 us -> 0.11 us
    ppermute x4, waiting for transfers between devices: 15.7 us -> 19.1 us  [on_device(): up_next = lax.ppermute(up_block, 'ad', forward)]
    convert_element_type x1, other arithmetic: 5.5 us -> 8.67 us  [on_device(): (wide_hidden * inv_rms * gain.astype(jnp.float32)).astype(jnp.bfloat16)]
    dynamic_slice x2 -> x0, local copies, waits for them, and re-layouts: 2.83 us -> none  [the longest x1 1.6 us: on_device(): from_behind = order_table[lax.rem(my_place + owners - step, owners)]]
    dot_general x2, matrix products: 5.75 us -> 4.11 us  [base_of(): jnp.dot(normed, part, preferred_element_type=jnp.float32)]
    dynamic_slice x1, local copies, waits for them, and re-layouts: 0.2 us -> 1.66 us  [on_device(): lax.dynamic_slice_in_dim(normed, lax.axis_index('tp') * column_portion, c...]
  transfers between devices with their start and end apart: 18 -> 18, of which waited for: 8 -> 10; matrix products, arithmetic and copies ran while one was open for 44% -> 40% of each run, Pallas kernels for 0% -> 0%
where the time goes in v4:
time: 111 us
  waiting for transfers between devices  43.8 us (39%)
  starting transfers between devices  19.1 us (17%)
  matrix products  17.5 us (16%)
  local copies, waits for them, and re-layouts  15.1 us (14%)
  other arithmetic  14.6 us (13%)
    ppermute x4, waiting for transfers between devices, on_device(): up_next = lax.ppermute(up_block, 'ad', forward)  19.1 us
    ppermute x4, waiting for transfers between devices, carry_up(): up_f = lax.ppermute(up_f, 'ad', forward)  14.9 us
    dot_general x16, matrix products, term(): low = jnp.dot(own_cols, block[j], preferred_element_type=jnp.float32)  12.4 us
    convert_element_type x1, other arithmetic, on_device(): (wide_hidden * inv_rms * gain.astype(jnp.float32)).astype(jnp.bfloat16)  8.67 us
    ppermute x4, starting transfers between devices, on_device(): up_next = lax.ppermute(up_block, 'ad', forward)  7.81 us
    optimization_barrier x1, local copies, waits for them, and re-layouts, tie(): return lax.optimization_barrier(values)  7.74 us
    ppermute x4, starting transfers between devices, carry_up(): up_f = lax.ppermute(up_f, 'ad', forward)  6.81 us
    ppermute x2, waiting for transfers between devices, sum_parts(): lax.ppermute(total.astype(jnp.bfloat16), 'tp', pairs).astype(jnp.float32)  4.9 us
  transfers between devices with their start and end apart: 18, of which 10 were waited for; matrix products, arithmetic and copies ran while one was open for 40% of the time, Pallas kernels for 0%

profile of v4, /device:TPU:0, one launch (start us, length us, event | category | flops | bytes accessed | tf_op | source)
XLA Modules:
  0.0 110.6 jit_solution(8353130579699010842)
XLA Ops:
  0.0 3.0 %collective-permute-start = (bf16[2,2048,128]{2,1,0:T(8,128)(2,1)}, bf16[2,2048,128]{2,1,0:T(8,128)(2,1)S(1)}, u32[]{:S(2)}, u32[]{:S(2)}) collective-permute-start(bf16[2,2048,128]{2,1,0:T(8,128)(2,1)} %param.10), channel_id=1, source_target_pairs={{0,2},{2,4},{4,6},{6,7},{7,5},{5,3},{3,1},{1,0},{8,10},{10,12},{12... | collective-permute-start | bytes 3145736 | tf_op jit(solution)/shard_map/ppermute | solution.py:104
  3.0 2.0 %collective-permute-start.2 = (bf16[2,2,64,256]{3,2,1,0:T(8,128)(2,1)}, bf16[2,2,64,256]{3,2,1,0:T(8,128)(2,1)S(1)}, u32[]{:S(2)}, u32[]{:S(2)}) collective-permute-start(bf16[2,2,64,256]{3,2,1,0:T(8,128)(2,1)} %param.11), channel_id=1, source_target_pairs={{0,2},{2,4},{4,6},{6,7},{7,5},{5,3},{3,1},{1,0},{8,10},{10,12},{12... | collective-permute-start | bytes 393224 | tf_op jit(solution)/shard_map/ppermute | solution.py:93
  5.2 0.7 convert_element_type.43
  5.9 4.6 %fusion = f32[448]{0:T(512)S(1)} fusion(bf16[448,8192]{1,0:T(8,128)(2,1)} %param.7), kind=kLoop, calls=%fused_computation.2 | loop fusion | flops 11009600 | bytes 7341824 | tf_op jit(solution)/shard_map/reduce_sum | solution.py:64
  10.5 0.0 copy-start.2
  10.5 0.0 copy-start.3
  10.5 8.7 %fusion.2 = bf16[448,8192]{1,0:T(8,128)(2,1)} fusion(bf16[448,8192]{1,0:T(8,128)(2,1)} %param.7, f32[8192]{0:T(1024)S(1)} %convert_element_type.43, f32[448]{0:T(512)S(1)} %add_rsqrt_fusion), kind=kLoop, calls=%fused_computation.4 | loop fusion | flops 14680064 | bytes 14714624 | tf_op jit(solution)/shard_map/convert_element_type | solution.py:65
  19.2 0.1 select_reduce_fusion
  19.3 0.1 concatenate.6
  19.4 0.1 broadcast_compare_fusion
  19.5 1.7 %constant_dynamic-slice_fusion = bf16[448,2048]{1,0:T(8,128)(2,1)S(1)} fusion(bf16[448,8192]{1,0:T(8,128)(2,1)} %fusion.2, s32[]{:T(128)S(6)} %select_n.128), kind=kLoop, calls=%fused_computation.117 | loop fusion | bytes 3670020 | tf_op jit(solution)/shard_map/dynamic_slice | solution.py:66
  21.2 7.9 %collective-permute-done.2 = bf16[2,2,64,256]{3,2,1,0:T(8,128)(2,1)S(1)} collective-permute-done((bf16[2,2,64,256]{3,2,1,0:T(8,128)(2,1)}, bf16[2,2,64,256]{3,2,1,0:T(8,128)(2,1)S(1)}, u32[]{:S(2)}, u32[]{:S(2)}) %collective-permute-start.2) | collective-permute-done | bytes 131104 | tf_op jit(solution)/shard_map/ppermute | solution.py:93
  29.2 1.5 %collective-permute-done.3 = bf16[2,2,64,256]{3,2,1,0:T(8,128)(2,1)S(1)} collective-permute-done((bf16[2,2,64,256]{3,2,1,0:T(8,128)(2,1)}, bf16[2,2,64,256]{3,2,1,0:T(8,128)(2,1)S(1)}, u32[]{:S(2)}, u32[]{:S(2)}) %collective-permute-start.3) | collective-permute-done | bytes 131104 | tf_op jit(solution)/shard_map/ppermute | solution.py:94
  30.7 1.6 %collective-permute-start.4 = (bf16[2,2048,128]{2,1,0:T(8,128)(2,1)S(1)}, bf16[2,2048,128]{2,1,0:T(8,128)(2,1)S(1)}, u32[]{:S(2)}, u32[]{:S(2)}) collective-permute-start(bf16[2,2048,128]{2,1,0:T(8,128)(2,1)S(1)} %collective-permute-done), channel_id=1, source_target_pairs={{0,2},{2,4},{4,6},{6,7},{7,5},{5,3},{3,1},{1,0},{8,10},{10,12},{12... | collective-permute-start | bytes 3145736 | tf_op jit(solution)/shard_map/ppermute | solution.py:104
  32.3 0.4 collective-permute-start.5
  32.8 7.7 %copy.14 = bf16[8192,2,256]{2,0,1:T(8,128)(2,1)} copy(bf16[8192,2,256]{2,1,0:T(2,128)(2,1)} %param.9) | data formatting | bytes 16777216 | tf_op jit(solution)/shard_map/optimization_barrier | solution.py:15
  40.5 3.8 %slice_bitcast_fusion = (bf16[8192,256]{1,0:T(8,128)(2,1)S(1)}, bf16[8192,256]{1,0:T(8,128)(2,1)S(1)}) fusion(bf16[8192,2,256]{2,0,1:T(8,128)(2,1)} %copy.14), kind=kLoop, calls=%fused_computation.5 | loop fusion | bytes 16777216 | tf_op jit(solution)/shard_map/squeeze | solution.py:109
  44.3 1.6 %collective-permute-start.6 = (bf16[2,2,64,256]{3,2,1,0:T(8,128)(2,1)S(1)}, bf16[2,2,64,256]{3,2,1,0:T(8,128)(2,1)S(1)}, u32[]{:S(2)}, u32[]{:S(2)}) collective-permute-start(bf16[2,2,64,256]{3,2,1,0:T(8,128)(2,1)S(1)} %collective-permute-done.2), channel_id=1, source_target_pairs={{0,2},{2,4},{4,6},{6,7},{7,5},{5,3},{3,1},{1,0},{8,10},{10,12},{12... | collective-permute-start | bytes 393224 | tf_op jit(solution)/shard_map/ppermute | solution.py:93
  45.9 0.4 collective-permute-start.7
  46.4 0.6 convolution_select_fusion.10
  47.0 0.6 convolution_select_fusion.14
  47.7 0.6 fusion.17
  48.4 0.6 convolution_select_fusion.12
  49.0 0.6 fusion.16
  49.7 0.6 fusion.14
  50.3 6.9 %collective-permute-done.6 = bf16[2,2,64,256]{3,2,1,0:T(8,128)(2,1)S(1)} collective-permute-done((bf16[2,2,64,256]{3,2,1,0:T(8,128)(2,1)S(1)}, bf16[2,2,64,256]{3,2,1,0:T(8,128)(2,1)S(1)}, u32[]{:S(2)}, u32[]{:S(2)}) %collective-permute-start.6) | collective-permute-done | bytes 131104 | tf_op jit(solution)/shard_map/ppermute | solution.py:93
  57.3 1.3 %collective-permute-done.7 = bf16[2,2,64,256]{3,2,1,0:T(8,128)(2,1)S(1)} collective-permute-done((bf16[2,2,64,256]{3,2,1,0:T(8,128)(2,1)S(1)}, bf16[2,2,64,256]{3,2,1,0:T(8,128)(2,1)S(1)}, u32[]{:S(2)}, u32[]{:S(2)}) %collective-permute-start.7) | collective-permute-done | bytes 131104 | tf_op jit(solution)/shard_map/ppermute | solution.py:94
  58.6 1.6 %collective-permute-start.10 = (bf16[2,2,64,256]{3,2,1,0:T(8,128)(2,1)S(1)}, bf16[2,2,64,256]{3,2,1,0:T(8,128)(2,1)S(1)}, u32[]{:S(2)}, u32[]{:S(2)}) collective-permute-start(bf16[2,2,64,256]{3,2,1,0:T(8,128)(2,1)S(1)} %collective-permute-done.6), channel_id=1, source_target_pairs={{0,2},{2,4},{4,6},{6,7},{7,5},{5,3},{3,1},{1,0},{8,10},{10,12},{12... | collective-permute-start | bytes 393224 | tf_op jit(solution)/shard_map/ppermute | solution.py:93
  60.2 0.4 collective-permute-start.11
  60.7 1.6 %collective-permute-start.8 = (bf16[2,2048,128]{2,1,0:T(8,128)(2,1)S(1)}, bf16[2,2048,128]{2,1,0:T(8,128)(2,1)S(1)}, u32[]{:S(2)}, u32[]{:S(2)}) collective-permute-start(bf16[2,2048,128]{2,1,0:T(8,128)(2,1)S(1)} %collective-permute-done.4), channel_id=1, source_target_pairs={{0,2},{2,4},{4,6},{6,7},{7,5},{5,3},{3,1},{1,0},{8,10},{10,12},{12... | collective-permute-start | bytes 3145736 | tf_op jit(solution)/shard_map/ppermute | solution.py:104
  62.3 0.4 collective-permute-start.9
  62.7 2.1 %fusion.57 = f32[448,256]{1,0:T(8,128)S(1)} fusion(bf16[448,8192]{1,0:T(8,128)(2,1)S(1)} %bitcast.91, bf16[8192,256]{1,0:T(8,128)(2,1)S(1)} %get-tuple-element.55), kind=kOutput, calls=%fused_computation.122 | convolution fusion | flops 1879048192 | bytes 11993088 | tf_op jit(solution)/shard_map/dot_general | solution.py:31
  64.8 2.1 %fusion.56 = f32[448,256]{1,0:T(8,128)S(1)} fusion(bf16[448,8192]{1,0:T(8,128)(2,1)S(1)} %bitcast.91, bf16[8192,256]{1,0:T(8,128)(2,1)S(1)} %get-tuple-element.54), kind=kOutput, calls=%fused_computation.121 | convolution fusion | flops 1879048192 | bytes 11993088 | tf_op jit(solution)/shard_map/dot_general | solution.py:31
  66.8 1.7 %convolution_select_fusion.6 = f32[448,128]{1,0:T(8,128)S(1)} fusion(bf16[448,2048]{1,0:T(8,128)(2,1)S(1)} %constant_dynamic-slice_fusion, bf16[2,2048,128]{2,1,0:T(8,128)(2,1)} %collective-permute-done.5, pred[448]{0:T(512)(128)(4,1)S(1)} %get-tuple-element.81), kind=kOutput, calls=%fused_computation.21 | convolution fusion | flops 234938368 | bytes 2589120 | tf_op jit(solution)/shard_map/dot_general | solution.py:74
  68.5 0.6 convolution_select_fusion.8
  69.2 0.6 fusion.12
  69.8 1.7 %fusion.10 = f32[448,128]{1,0:T(8,128)S(1)} fusion(f32[448,128]{1,0:T(8,128)S(1)} %fusion.12, f32[448,128]{1,0:T(8,128)S(1)} %convolution_select_fusion.6, bf16[448,2048]{1,0:T(8,128)(2,1)S(1)} %constant_dynamic-slice_fusion, bf16[2,2048,128]{2,1,0:T(8,128)(2,1)} %collective-permute-done.5, pred[448]{0:T(512)(128)(4,1)S(1)} %get-tuple-element.82), kind=kOutput, calls=%fused_computation.24 | convolution fusion | flops 235053056 | bytes 3047872 | tf_op jit(solution)/shard_map/dot_general | solution.py:74
  71.6 12.5 %collective-permute-done.8 = bf16[2,2048,128]{2,1,0:T(8,128)(2,1)S(1)} collective-permute-done((bf16[2,2048,128]{2,1,0:T(8,128)(2,1)S(1)}, bf16[2,2048,128]{2,1,0:T(8,128)(2,1)S(1)}, u32[]{:S(2)}, u32[]{:S(2)}) %collective-permute-start.8) | collective-permute-done | bytes 1048608 | tf_op jit(solution)/shard_map/ppermute | solution.py:104
  84.1 1.5 %collective-permute-done.9 = bf16[2,2048,128]{2,1,0:T(8,128)(2,1)S(1)} collective-permute-done((bf16[2,2048,128]{2,1,0:T(8,128)(2,1)}, bf16[2,2048,128]{2,1,0:T(8,128)(2,1)S(1)}, u32[]{:S(2)}, u32[]{:S(2)}) %collective-permute-start.9) | collective-permute-done | bytes 1048608 | tf_op jit(solution)/shard_map/ppermute | solution.py:105
  85.7 1.5 %collective-permute-start.16 = (bf16[1,2,64,256]{3,2,1,0:T(8,128)(2,1)S(1)}, bf16[1,2,64,256]{3,2,1,0:T(8,128)(2,1)S(1)}, u32[]{:S(2)}, u32[]{:S(2)}) collective-permute-start(bf16[1,2,64,256]{3,2,1,0:T(8,128)(2,1)S(1)} %slice.91), channel_id=1, source_target_pairs={{0,2},{2,4},{4,6},{6,7},{7,5},{5,3},{3,1},{1,0},{8,10},{10,12},{12... | collective-permute-start | bytes 196616 | tf_op jit(solution)/shard_map/ppermute | solution.py:93
  87.2 0.5 collective-permute-start.17
  87.7 0.6 convolution_select_fusion.4
  88.4 1.6 %collective-permute-start.12 = (bf16[1,2048,128]{2,1,0:T(8,128)(2,1)S(1)}, bf16[1,2048,128]{2,1,0:T(8,128)(2,1)S(1)}, u32[]{:S(2)}, u32[]{:S(2)}) collective-permute-start(bf16[1,2048,128]{2,1,0:T(8,128)(2,1)S(1)} %slice.88), channel_id=1, source_target_pairs={{0,2},{2,4},{4,6},{6,7},{7,5},{5,3},{3,1},{1,0},{8,10},{10,12},{12... | collective-permute-start | bytes 1572872 | tf_op jit(solution)/shard_map/ppermute | solution.py:104
  90.0 0.6 collective-permute-start.13
  90.6 0.6 fusion.8
  91.2 0.6 convolution_select_fusion.2
  91.9 0.7 fusion.7
  92.5 6.5 %collective-permute-done.12 = bf16[1,2048,128]{2,1,0:T(8,128)(2,1)S(1)} collective-permute-done((bf16[1,2048,128]{2,1,0:T(8,128)(2,1)S(1)}, bf16[1,2048,128]{2,1,0:T(8,128)(2,1)S(1)}, u32[]{:S(2)}, u32[]{:S(2)}) %collective-permute-start.12) | collective-permute-done | bytes 524320 | tf_op jit(solution)/shard_map/ppermute | solution.py:104
  99.0 0.6 convolution_select_fusion.1
  99.7 0.7 collective-permute-done.13
  100.4 0.6 fusion.55
  101.0 0.1 collective-permute-start.14
  101.1 1.3 %collective-permute-done.14 = bf16[448,128]{1,0:T(8,128)(2,1)S(1)} collective-permute-done((bf16[448,128]{1,0:T(8,128)(2,1)S(1)}, bf16[448,128]{1,0:T(8,128)(2,1)S(1)}, u32[]{:S(2)}, u32[]{:S(2)}) %collective-permute-start.14) | collective-permute-done | bytes 114720 | tf_op jit(solution)/shard_map/ppermute | solution.py:25
  102.4 1.6 %collective-permute-start.15 = (bf16[448,128]{1,0:T(8,128)(2,1)S(1)}, bf16[448,128]{1,0:T(8,128)(2,1)S(1)}, u32[]{:S(2)}, u32[]{:S(2)}) collective-permute-start(bf16[448,128]{1,0:T(8,128)(2,1)S(1)} %fusion.50), channel_id=1, source_target_pairs={{0,16},{8,24},{16,0},{24,8},{1,17},{9,25},{17,1},{25,9},{2,18},{10... | collective-permute-start | bytes 344072 | tf_op jit(solution)/shard_map/ppermute | solution.py:25
  104.0 0.1 fusion.53
  104.1 3.6 %collective-permute-done.15 = bf16[448,128]{1,0:T(8,128)(2,1)S(1)} collective-permute-done((bf16[448,128]{1,0:T(8,128)(2,1)S(1)}, bf16[448,128]{1,0:T(8,128)(2,1)S(1)}, u32[]{:S(2)}, u32[]{:S(2)}) %collective-permute-start.15) | collective-permute-done | bytes 114720 | tf_op jit(solution)/shard_map/ppermute | solution.py:25
  107.8 0.1 fusion.54
  107.9 0.1 copy.16
  108.0 0.1 copy.17
  108.1 0.1 broadcast_select_fusion.1
  108.2 0.5 fusion.4
  108.7 0.5 fusion.6
  109.1 0.1 fusion.48
  109.4 1.2 %copy.18 = bf16[448,2,256]{2,1,0:T(2,128)(2,1)} copy(bf16[448,2,256]{2,0,1:T(8,128)(2,1)S(1)} %pad_maximum_fusion) | data formatting | bytes 917504 | tf_op jit(solution)/shard_map/stack | solution.py:158
  (46 shorter events, 0.4 us)
Async XLA Ops:
  0.0 30.7 %collective-permute-start = (bf16[2,2048,128]{2,1,0:T(8,128)(2,1)}, bf16[2,2048,128]{2,1,0:T(8,128)(2,1)S(1)}, u32[]{:S(2)}, u32[]{:S(2)}) collective-permute-start(bf16[2,2048,128]{2,1,0:T(8,128)(2,1)} %param.10), channel_id=1, source_target_pairs={{0,2},{2,4},{4,6},{6,7},{7,5},{5,3},{3,1},{1,0},{8,10},{10,12},{12... | collective-permute-start | bytes 3145736 | tf_op jit(solution)/shard_map/ppermute | solution.py:104
  3.0 27.7 %collective-permute-start.1 = (bf16[2,2048,128]{2,1,0:T(8,128)(2,1)}, bf16[2,2048,128]{2,1,0:T(8,128)(2,1)S(1)}, u32[]{:S(2)}, u32[]{:S(2)}) collective-permute-start(bf16[2,2048,128]{2,1,0:T(8,128)(2,1)} %param.10), channel_id=1, source_target_pairs={{2,0},{4,2},{6,4},{7,6},{5,7},{3,5},{1,3},{0,1},{10,8},{12,10},{14... | collective-permute-start | bytes 3145736 | tf_op jit(solution)/shard_map/ppermute | solution.py:105
  3.0 26.1 %collective-permute-start.2 = (bf16[2,2,64,256]{3,2,1,0:T(8,128)(2,1)}, bf16[2,2,64,256]{3,2,1,0:T(8,128)(2,1)S(1)}, u32[]{:S(2)}, u32[]{:S(2)}) collective-permute-start(bf16[2,2,64,256]{3,2,1,0:T(8,128)(2,1)} %param.11), channel_id=1, source_target_pairs={{0,2},{2,4},{4,6},{6,7},{7,5},{5,3},{3,1},{1,0},{8,10},{10,12},{12... | collective-permute-start | bytes 393224 | tf_op jit(solution)/shard_map/ppermute | solution.py:93
  5.1 25.6 %collective-permute-start.3 = (bf16[2,2,64,256]{3,2,1,0:T(8,128)(2,1)}, bf16[2,2,64,256]{3,2,1,0:T(8,128)(2,1)S(1)}, u32[]{:S(2)}, u32[]{:S(2)}) collective-permute-start(bf16[2,2,64,256]{3,2,1,0:T(8,128)(2,1)} %param.11), channel_id=1, source_target_pairs={{2,0},{4,2},{6,4},{7,6},{5,7},{3,5},{1,3},{0,1},{10,8},{12,10},{14... | collective-permute-start | bytes 393224 | tf_op jit(solution)/shard_map/ppermute | solution.py:94
  10.5 8.7 %copy-start.2 = (s32[448]{0:T(512)S(1)}, s32[448]{0:T(512)}, u32[]{:S(2)}) copy-start(s32[448]{0:T(512)} %param.12) | copy-start | bytes 5380
  10.5 8.7 %copy-start.3 = (s32[16]{0:T(128)S(1)}, s32[16]{0:T(128)}, u32[]{:S(2)}) copy-start(s32[16]{0:T(128)} %param.13) | copy-start | bytes 196
  19.5 1.7 %copy-start.1 = (bf16[2,2,64,256]{3,2,1,0:T(8,128)(2,1)S(1)}, bf16[2,2,64,256]{3,2,1,0:T(8,128)(2,1)}, u32[]{:S(2)}) copy-start(bf16[2,2,64,256]{3,2,1,0:T(8,128)(2,1)} %param.11) | copy-start | bytes 393220
  30.7 27.9 %collective-permute-start.4 = (bf16[2,2048,128]{2,1,0:T(8,128)(2,1)S(1)}, bf16[2,2048,128]{2,1,0:T(8,128)(2,1)S(1)}, u32[]{:S(2)}, u32[]{:S(2)}) collective-permute-start(bf16[2,2048,128]{2,1,0:T(8,128)(2,1)S(1)} %collective-permute-done), channel_id=1, source_target_pairs={{0,2},{2,4},{4,6},{6,7},{7,5},{5,3},{3,1},{1,0},{8,10},{10,12},{12... | collective-permute-start | bytes 3145736 | tf_op jit(solution)/shard_map/ppermute | solution.py:104
  32.3 26.3 %collective-permute-start.5 = (bf16[2,2048,128]{2,1,0:T(8,128)(2,1)S(1)}, bf16[2,2048,128]{2,1,0:T(8,128)(2,1)}, u32[]{:S(2)}, u32[]{:S(2)}) collective-permute-start(bf16[2,2048,128]{2,1,0:T(8,128)(2,1)S(1)} %collective-permute-done.1), channel_id=1, source_target_pairs={{2,0},{4,2},{6,4},{7,6},{5,7},{3,5},{1,3},{0,1},{10,8},{12,10},{14... | collective-permute-start | bytes 3145736 | tf_op jit(solution)/shard_map/ppermute | solution.py:105
  44.3 2.7 %copy-start = (bf16[2,2048,128]{2,1,0:T(8,128)(2,1)S(1)}, bf16[2,2048,128]{2,1,0:T(8,128)(2,1)}, u32[]{:S(2)}) copy-start(bf16[2,2048,128]{2,1,0:T(8,128)(2,1)} %param.10) | copy-start | bytes 3145732
  44.3 13.0 %collective-permute-start.6 = (bf16[2,2,64,256]{3,2,1,0:T(8,128)(2,1)S(1)}, bf16[2,2,64,256]{3,2,1,0:T(8,128)(2,1)S(1)}, u32[]{:S(2)}, u32[]{:S(2)}) collective-permute-start(bf16[2,2,64,256]{3,2,1,0:T(8,128)(2,1)S(1)} %collective-permute-done.2), channel_id=1, source_target_pairs={{0,2},{2,4},{4,6},{6,7},{7,5},{5,3},{3,1},{1,0},{8,10},{10,12},{12... | collective-permute-start | bytes 393224 | tf_op jit(solution)/shard_map/ppermute | solution.py:93
  45.9 12.6 %collective-permute-start.7 = (bf16[2,2,64,256]{3,2,1,0:T(8,128)(2,1)S(1)}, bf16[2,2,64,256]{3,2,1,0:T(8,128)(2,1)S(1)}, u32[]{:S(2)}, u32[]{:S(2)}) collective-permute-start(bf16[2,2,64,256]{3,2,1,0:T(8,128)(2,1)S(1)} %collective-permute-done.3), channel_id=1, source_target_pairs={{2,0},{4,2},{6,4},{7,6},{5,7},{3,5},{1,3},{0,1},{10,8},{12,10},{14... | collective-permute-start | bytes 393224 | tf_op jit(solution)/shard_map/ppermute | solution.py:94
  47.0 15.7 %slice-start = ((s8[7340032]{0:T(1024)(128)(4,1)}), s8[4194304]{0:T(1024)(128)(4,1)S(1)}, s32[]{:S(2)}) async-start(s8[7340032]{0:T(1024)(128)(4,1)} %bitcast.90), calls=%async_computation | async-start | bytes 8388608
  48.4 14.4 %slice-start.1 = ((s8[7340032]{0:T(1024)(128)(4,1)}), s8[3145728]{0:T(1024)(128)(4,1)S(1)}, s32[]{:S(2)}) async-start(s8[7340032]{0:T(1024)(128)(4,1)} %bitcast.90), calls=%async_computation.1 | async-start | bytes 6291456
  58.6 12.9 %collective-permute-start.10 = (bf16[2,2,64,256]{3,2,1,0:T(8,128)(2,1)S(1)}, bf16[2,2,64,256]{3,2,1,0:T(8,128)(2,1)S(1)}, u32[]{:S(2)}, u32[]{:S(2)}) collective-permute-start(bf16[2,2,64,256]{3,2,1,0:T(8,128)(2,1)S(1)} %collective-permute-done.6), channel_id=1, source_target_pairs={{0,2},{2,4},{4,6},{6,7},{7,5},{5,3},{3,1},{1,0},{8,10},{10,12},{12... | collective-permute-start | bytes 393224 | tf_op jit(solution)/shard_map/ppermute | solution.py:93
  60.2 11.3 %collective-permute-start.11 = (bf16[2,2,64,256]{3,2,1,0:T(8,128)(2,1)S(1)}, bf16[2,2,64,256]{3,2,1,0:T(8,128)(2,1)S(1)}, u32[]{:S(2)}, u32[]{:S(2)}) collective-permute-start(bf16[2,2,64,256]{3,2,1,0:T(8,128)(2,1)S(1)} %collective-permute-done.7), channel_id=1, source_target_pairs={{2,0},{4,2},{6,4},{7,6},{5,7},{3,5},{1,3},{0,1},{10,8},{12,10},{14... | collective-permute-start | bytes 393224 | tf_op jit(solution)/shard_map/ppermute | solution.py:94
  60.7 23.5 %collective-permute-start.8 = (bf16[2,2048,128]{2,1,0:T(8,128)(2,1)S(1)}, bf16[2,2048,128]{2,1,0:T(8,128)(2,1)S(1)}, u32[]{:S(2)}, u32[]{:S(2)}) collective-permute-start(bf16[2,2048,128]{2,1,0:T(8,128)(2,1)S(1)} %collective-permute-done.4), channel_id=1, source_target_pairs={{0,2},{2,4},{4,6},{6,7},{7,5},{5,3},{3,1},{1,0},{8,10},{10,12},{12... | collective-permute-start | bytes 3145736 | tf_op jit(solution)/shard_map/ppermute | solution.py:104
  62.3 23.4 %collective-permute-start.9 = (bf16[2,2048,128]{2,1,0:T(8,128)(2,1)}, bf16[2,2048,128]{2,1,0:T(8,128)(2,1)S(1)}, u32[]{:S(2)}, u32[]{:S(2)}) collective-permute-start(bf16[2,2048,128]{2,1,0:T(8,128)(2,1)} %collective-permute-done.5), channel_id=1, source_target_pairs={{2,0},{4,2},{6,4},{7,6},{5,7},{3,5},{1,3},{0,1},{10,8},{12,10},{14... | collective-permute-start | bytes 3145736 | tf_op jit(solution)/shard_map/ppermute | solution.py:105
  85.7 15.4 %collective-permute-start.16 = (bf16[1,2,64,256]{3,2,1,0:T(8,128)(2,1)S(1)}, bf16[1,2,64,256]{3,2,1,0:T(8,128)(2,1)S(1)}, u32[]{:S(2)}, u32[]{:S(2)}) collective-permute-start(bf16[1,2,64,256]{3,2,1,0:T(8,128)(2,1)S(1)} %slice.91), channel_id=1, source_target_pairs={{0,2},{2,4},{4,6},{6,7},{7,5},{5,3},{3,1},{1,0},{8,10},{10,12},{12... | collective-permute-start | bytes 196616 | tf_op jit(solution)/shard_map/ppermute | solution.py:93
  87.2 13.9 %collective-permute-start.17 = (bf16[1,2,64,256]{3,2,1,0:T(8,128)(2,1)S(1)}, bf16[1,2,64,256]{3,2,1,0:T(8,128)(2,1)S(1)}, u32[]{:S(2)}, u32[]{:S(2)}) collective-permute-start(bf16[1,2,64,256]{3,2,1,0:T(8,128)(2,1)S(1)} %slice.92), channel_id=1, source_target_pairs={{2,0},{4,2},{6,4},{7,6},{5,7},{3,5},{1,3},{0,1},{10,8},{12,10},{14... | collective-permute-start | bytes 196616 | tf_op jit(solution)/shard_map/ppermute | solution.py:94
  88.4 10.6 %collective-permute-start.12 = (bf16[1,2048,128]{2,1,0:T(8,128)(2,1)S(1)}, bf16[1,2048,128]{2,1,0:T(8,128)(2,1)S(1)}, u32[]{:S(2)}, u32[]{:S(2)}) collective-permute-start(bf16[1,2048,128]{2,1,0:T(8,128)(2,1)S(1)} %slice.88), channel_id=1, source_target_pairs={{0,2},{2,4},{4,6},{6,7},{7,5},{5,3},{3,1},{1,0},{8,10},{10,12},{12... | collective-permute-start | bytes 1572872 | tf_op jit(solution)/shard_map/ppermute | solution.py:104
  90.0 10.4 %collective-permute-start.13 = (bf16[1,2048,128]{2,1,0:T(8,128)(2,1)S(1)}, bf16[1,2048,128]{2,1,0:T(8,128)(2,1)S(1)}, u32[]{:S(2)}, u32[]{:S(2)}) collective-permute-start(bf16[1,2048,128]{2,1,0:T(8,128)(2,1)S(1)} %slice.89), channel_id=1, source_target_pairs={{2,0},{4,2},{6,4},{7,6},{5,7},{3,5},{1,3},{0,1},{10,8},{12,10},{14... | collective-permute-start | bytes 1572872 | tf_op jit(solution)/shard_map/ppermute | solution.py:105
  101.0 1.4 %collective-permute-start.14 = (bf16[448,128]{1,0:T(8,128)(2,1)S(1)}, bf16[448,128]{1,0:T(8,128)(2,1)S(1)}, u32[]{:S(2)}, u32[]{:S(2)}) collective-permute-start(bf16[448,128]{1,0:T(8,128)(2,1)S(1)} %get-tuple-element.91), channel_id=1, source_target_pairs={{0,8},{8,0},{16,24},{24,16},{1,9},{9,1},{17,25},{25,17},{2,10},{10... | collective-permute-start | bytes 344072 | tf_op jit(solution)/shard_map/ppermute | solution.py:25
  102.4 5.3 %collective-permute-start.15 = (bf16[448,128]{1,0:T(8,128)(2,1)S(1)}, bf16[448,128]{1,0:T(8,128)(2,1)S(1)}, u32[]{:S(2)}, u32[]{:S(2)}) collective-permute-start(bf16[448,128]{1,0:T(8,128)(2,1)S(1)} %fusion.50), channel_id=1, source_target_pairs={{0,16},{8,24},{16,0},{24,8},{1,17},{9,25},{17,1},{25,9},{2,18},{10... | collective-permute-start | bytes 344072 | tf_op jit(solution)/shard_map/ppermute | solution.py:25
